TPU v7x, 128 devices: a whole 4x4x4 slice. The times are simulated.
128 devices in a mesh: dp: 16 (over z, y_hi, core), tensor: 8 (over y_lo, x).
Axes of the slice: x: 4, y: 4 (y_hi: 2, y_lo: 2; y = y_hi * 2 + y_lo), z: 4, core: 2. Of those that a mesh axis runs over, the one named last changes fastest.
Arguments:
- tokens: bfloat16 [16384, 1024], P(('dp', 'tensor')), may hold values from -6 to 6
- qkv_weight: bfloat16 [2, 1024, 3, 1024], P(None, 'dp', None, 'tensor'), may hold values from -0.1875 to 0.1875
- qkv_bias: bfloat16 [2, 3, 1024], P(None, None, 'tensor'), may hold values from -0.59765625 to 0.59765625
- out_weight: bfloat16 [2, 1024, 1024], P(None, 'dp', 'tensor'), may hold values from -0.75 to 0.75
- up_weight: bfloat16 [2, 1024, 4096], P(None, 'dp', 'tensor'), may hold values from -0.1875 to 0.1875
- up_bias: bfloat16 [2, 4096], P(None, 'tensor'), may hold values from -3 to 3
- down_weight: bfloat16 [2, 1024, 4096], P(None, 'dp', 'tensor'), may hold values from -0.09375 to 0.09375
- norm_gain: bfloat16 [2, 2, 1024], replicated, may hold values from 0.5 to 1.5
- norm_shift: bfloat16 [2, 2, 1024], replicated, may hold values from -1.796875 to 1.796875
- out_bias: bfloat16 [2, 1024], replicated, may hold values from -3 to 3
- cotangent: bfloat16 [16384, 1024], P(('dp', 'tensor')), may hold values from -6 to 6
Outputs:
- output: bfloat16 [16384, 1024], P(('dp', 'tensor'))
- tokens_grad: float32 [16384, 1024], P(('dp', 'tensor'))
- qkv_weight_grad: float32 [2, 1024, 3, 1024], P(None, 'dp', None, 'tensor')
- qkv_bias_grad: float32 [2, 3, 1024], P(None, None, 'tensor')
- out_weight_grad: float32 [2, 1024, 1024], P(None, 'dp', 'tensor')
- up_weight_grad: float32 [2, 1024, 4096], P(None, 'dp', 'tensor')
- up_bias_grad: float32 [2, 4096], P(None, 'tensor')
- down_weight_grad: float32 [2, 1024, 4096], P(None, 'dp', 'tensor')
- norm_gain_grad: float32 [2, 2, 1024], replicated
- norm_shift_grad: float32 [2, 2, 1024], replicated
- out_bias_grad: float32 [2, 1024], replicated
All inputs are finite; a program needn't handle non-finite values.
Results may differ from a plain program's by a relative error of at most 0.02.
Values may be sent and summed in bfloat16 or wider, within the bound.
A program may use at most 128 MiB of HBM per device.

v0:
```python
from functools import partial

import jax
import jax.numpy as jnp
from jax import lax
from jax.sharding import PartitionSpec as P

D = 1024
HD = 64
ROT = 16
LAYERS = 2
SEQ_MIN = 2048


EPS = 1e-05
MASKED = -1e30


def shifted(value, axis, steps):
    count = lax.axis_size(axis)
    initial, last = (max(0, -steps), min(count, count - steps))
    return lax.ppermute(value, axis, [(source, source + steps) for source in range(initial, last)])


def norm_pair(residual, gain_pair, shift_pair):
    center_mean = jnp.mean(residual, axis=1, keepdims=True)
    centered = residual - center_mean
    variance = jnp.mean(centered * centered, axis=1, keepdims=True)
    normed = centered * lax.rsqrt(variance + EPS)
    return (normed * gain_pair[0] + shift_pair[0], normed * gain_pair[1] + shift_pair[1])


def rotary_turn(heads_in, positions):
    frequency = 10000.0 ** (-(jnp.arange(ROT // 2, dtype=jnp.float32) * 2.0) / ROT)
    angles = positions.astype(jnp.float32)[:, None] * frequency[None, :]
    angles = jnp.concatenate([angles, angles], axis=1)
    cosine = jnp.cos(angles)[:, None, :]
    sine_part = jnp.sin(angles)[:, None, :]
    rotary = heads_in[..., :ROT]
    halfway = ROT // 2
    turned = jnp.concatenate([-rotary[..., halfway:], rotary[..., :halfway]], axis=-1)
    return jnp.concatenate([rotary * cosine + turned * sine_part, heads_in[..., ROT:]], axis=-1)


def gelu_exact(values_in):
    return jax.nn.gelu(values_in, approximate=False)


def masked_scores(query_part, key_rows, query_pos, key_pos):
    scores = jnp.einsum(
        "qhd,khd->hqk", query_part, key_rows, preferred_element_type=jnp.float32
    ) * HD ** (-0.5)
    allowed = (query_pos[:, None] >= key_pos[None, :]) & (key_pos[None, :] >= 0)
    return jnp.where(allowed[None], scores, MASKED)


def attention_forward(queries, key_rows, value_rows, positions, key_pos):
    row_count, head_count = (queries.shape[0], queries.shape[1])
    block_rows = min(512, row_count)
    block_count = row_count // block_rows

    def one_block(pieces):
        query_part, query_pos = pieces
        scores = masked_scores(query_part, key_rows, query_pos, key_pos)
        row_max = jnp.max(scores, axis=2, keepdims=True)
        weights = jnp.exp(scores - row_max)
        totals = jnp.sum(weights, axis=2, keepdims=True)
        probs_low = (weights / totals).astype(jnp.bfloat16)
        block_out = jnp.einsum(
            "hqk,khd->qhd", probs_low, value_rows, preferred_element_type=jnp.float32
        )
        return (block_out, (row_max + jnp.log(totals))[:, :, 0])

    outputs, log_totals = lax.map(
        one_block,
        (
            queries.reshape(block_count, block_rows, head_count, HD),
            positions.reshape(block_count, block_rows),
        ),
    )
    return (outputs.reshape(row_count, head_count * HD), log_totals)


def attention_backward(
    queries, key_rows, value_rows, positions, key_pos, log_totals, attended_grad
):
    row_count, head_count = (queries.shape[0], queries.shape[1])
    block_rows = min(512, row_count)
    block_count = row_count // block_rows
    scale = HD ** (-0.5)

    def one_block(carried, pieces):
        key_grad, value_grad = carried
        query_part, query_pos, log_part, grad_part = pieces
        scores = masked_scores(query_part, key_rows, query_pos, key_pos)
        probs = jnp.exp(scores - log_part[:, :, None])
        value_grad = value_grad + jnp.einsum(
            "hqk,qhd->khd",
            probs.astype(jnp.bfloat16),
            grad_part,
            preferred_element_type=jnp.float32,
        )
        probs_grad = jnp.einsum(
            "qhd,khd->hqk", grad_part, value_rows, preferred_element_type=jnp.float32
        )
        weighted = jnp.sum(probs_grad * probs, axis=2, keepdims=True)
        scores_grad = (probs * (probs_grad - weighted)).astype(jnp.bfloat16)
        query_grad = (
            jnp.einsum("hqk,khd->qhd", scores_grad, key_rows, preferred_element_type=jnp.float32)
            * scale
        )
        key_grad = (
            key_grad
            + jnp.einsum(
                "hqk,qhd->khd", scores_grad, query_part, preferred_element_type=jnp.float32
            )
            * scale
        )
        return ((key_grad, value_grad), query_grad)

    zeros_start = jnp.zeros(key_rows.shape, jnp.float32)
    (key_grad, value_grad), query_grad = lax.scan(
        one_block,
        (zeros_start, zeros_start),
        (
            queries.reshape(block_count, block_rows, head_count, HD),
            positions.reshape(block_count, block_rows),
            log_totals,
            attended_grad.reshape(block_count, block_rows, head_count, HD),
        ),
    )
    return (query_grad.reshape(row_count, head_count, HD), key_grad, value_grad)


def partner_rows(stacked):
    earlier = shifted(stacked, "dp", 1 << 0)
    stacked = jnp.concatenate([earlier, stacked], axis=1)
    return stacked


def return_rows(stacked, seq_span):
    for bit_index in reversed(range(seq_span.bit_length() - 1)):
        halfway = stacked.shape[1] // 2
        front_part = stacked[:, :halfway]
        own_part = stacked[:, halfway:]
        stacked = own_part + shifted(
            front_part.astype(jnp.bfloat16), "dp", -(1 << bit_index)
        ).astype(front_part.dtype)
    return stacked


def branch_rows(attended, activated, out_rows, down_rows):
    contract_cols = (((1,), (1,)), ((), ()))
    return lax.dot_general(
        attended, out_rows, contract_cols, preferred_element_type=jnp.float32
    ) + lax.dot_general(activated, down_rows, contract_cols, preferred_element_type=jnp.float32)


def local(
    tokens,
    qkv_weight,
    qkv_bias,
    out_weight,
    up_weight,
    up_bias,
    down_weight,
    norm_gain,
    norm_shift,
    out_bias,
    cotangent,
):
    tensor_count = lax.axis_size("tensor")
    local_count = tokens.shape[0]
    row_count = local_count * tensor_count
    seq_span = max(SEQ_MIN, 2 * row_count) // row_count
    device_place = lax.axis_index("dp") % seq_span
    positions = device_place * row_count + jnp.arange(row_count, dtype=jnp.int32)
    key_pos = (device_place - seq_span + 1) * row_count + jnp.arange(
        seq_span * row_count, dtype=jnp.int32
    )
    head_count = qkv_bias.shape[2] // HD
    head_width = head_count * HD
    norm_gains = norm_gain.astype(jnp.float32)
    norm_shifts = norm_shift.astype(jnp.float32)
    contract_rows = (((0,), (0,)), ((), ()))
    contract_cols = (((1,), (1,)), ((), ()))
    residual = tokens.astype(jnp.float32)
    saved_layers = []
    for layer_index in range(LAYERS):
        gathered = (
            lax.all_gather(qkv_weight[layer_index], "dp", axis=0, tiled=True),
            lax.all_gather(out_weight[layer_index], "dp", axis=0, tiled=True),
            lax.all_gather(up_weight[layer_index], "dp", axis=0, tiled=True),
            lax.all_gather(down_weight[layer_index], "dp", axis=0, tiled=True),
        )
        attn_in, mlp_in = norm_pair(residual, norm_gains[layer_index], norm_shifts[layer_index])
        attn_rows, mlp_rows = (
            lax.all_gather(attn_in.astype(jnp.bfloat16), "tensor", axis=0, tiled=True),
            lax.all_gather(mlp_in.astype(jnp.bfloat16), "tensor", axis=0, tiled=True),
        )
        projected = jnp.dot(
            attn_rows, gathered[0].reshape(D, 3 * head_width), preferred_element_type=jnp.float32
        )
        projected = (
            projected + qkv_bias[layer_index].astype(jnp.float32).reshape(3 * head_width)
        ).reshape(row_count, 3, head_count, HD)
        queries = rotary_turn(projected[:, 0], positions).astype(jnp.bfloat16)
        own_keys = rotary_turn(projected[:, 1], positions).astype(jnp.bfloat16)
        own_values = projected[:, 2].astype(jnp.bfloat16)
        stacked = jnp.stack(
            [own_keys.reshape(row_count, head_width), own_values.reshape(row_count, head_width)]
        )
        stacked = partner_rows(stacked)
        key_rows = stacked[0].reshape(-1, head_count, HD)
        value_rows = stacked[1].reshape(-1, head_count, HD)
        attended, log_totals = attention_forward(queries, key_rows, value_rows, positions, key_pos)
        attended = attended.astype(jnp.bfloat16)
        hidden = jnp.dot(mlp_rows, gathered[2], preferred_element_type=jnp.float32) + up_bias[
            layer_index
        ].astype(jnp.float32)
        activated = gelu_exact(hidden).astype(jnp.bfloat16)
        branch = lax.psum_scatter(
            branch_rows(attended, activated, gathered[1], gathered[3]).astype(jnp.bfloat16),
            "tensor",
            scatter_dimension=0,
            tiled=True,
        ).astype(jnp.float32)
        kept_weights = None
        saved_layers.append(
            (
                residual,
                attn_rows,
                mlp_rows,
                queries,
                key_rows,
                value_rows,
                log_totals,
                attended,
                hidden,
                activated,
                kept_weights,
            )
        )
        residual = residual + branch + out_bias[layer_index].astype(jnp.float32)
    output = residual.astype(jnp.bfloat16)
    resid_grad = cotangent.astype(jnp.float32)
    weight_terms = [None] * LAYERS
    qkv_bias_terms = [None] * LAYERS
    up_bias_terms = [None] * LAYERS
    gain_terms = [None] * LAYERS
    shift_terms = [None] * LAYERS
    out_bias_terms = [None] * LAYERS
    for layer_index in reversed(range(LAYERS)):
        (
            layer_in,
            attn_rows,
            mlp_rows,
            queries,
            key_rows,
            value_rows,
            log_totals,
            attended,
            hidden,
            activated,
            kept_weights,
        ) = saved_layers[layer_index]
        gathered = (
            lax.all_gather(qkv_weight[layer_index], "dp", axis=0, tiled=True),
            lax.all_gather(out_weight[layer_index], "dp", axis=0, tiled=True),
            lax.all_gather(up_weight[layer_index], "dp", axis=0, tiled=True),
            lax.all_gather(down_weight[layer_index], "dp", axis=0, tiled=True),
        )
        out_bias_terms[layer_index] = jnp.sum(resid_grad, axis=0)
        grad_rows = lax.all_gather(resid_grad.astype(jnp.bfloat16), "tensor", axis=0, tiled=True)
        out_grad = lax.dot_general(
            grad_rows, attended, contract_rows, preferred_element_type=jnp.float32
        )
        down_grad = lax.dot_general(
            grad_rows, activated, contract_rows, preferred_element_type=jnp.float32
        )
        attended_grad = jnp.dot(grad_rows, gathered[1], preferred_element_type=jnp.float32).astype(
            jnp.bfloat16
        )
        activated_grad = lax.optimization_barrier(
            jnp.dot(grad_rows, gathered[3], preferred_element_type=jnp.float32).astype(jnp.bfloat16)
        ).astype(jnp.float32)
        gelu_back = jax.vjp(gelu_exact, hidden)[1]
        hidden_grad = gelu_back(activated_grad)[0].astype(jnp.bfloat16)
        up_grad = lax.dot_general(
            mlp_rows, hidden_grad, contract_rows, preferred_element_type=jnp.float32
        )
        up_bias_terms[layer_index] = jnp.sum(hidden_grad.astype(jnp.float32), axis=0)
        mlp_in_grad = lax.dot_general(
            hidden_grad, gathered[2], contract_cols, preferred_element_type=jnp.float32
        )
        query_grad, key_grad, value_grad = attention_backward(
            queries,
            key_rows,
            value_rows,
            positions,
            key_pos,
            log_totals,
            attended_grad.reshape(row_count, head_count, HD),
        )
        returned = return_rows(
            jnp.stack([key_grad.reshape(-1, head_width), value_grad.reshape(-1, head_width)]),
            seq_span,
        )
        rotary_back = jax.vjp(
            partial(rotary_turn, positions=positions),
            jnp.zeros((row_count, head_count, HD), jnp.float32),
        )[1]
        projected_grad = jnp.stack(
            [
                rotary_back(query_grad)[0],
                rotary_back(returned[0].reshape(row_count, head_count, HD))[0],
                returned[1].reshape(row_count, head_count, HD),
            ],
            axis=1,
        )
        projected_grad = projected_grad.astype(jnp.bfloat16).reshape(row_count, 3 * head_width)
        qkv_grad = lax.dot_general(
            attn_rows, projected_grad, contract_rows, preferred_element_type=jnp.float32
        ).reshape(D, 3, head_width)
        qkv_bias_terms[layer_index] = jnp.sum(projected_grad.astype(jnp.float32), axis=0).reshape(
            3, head_width
        )
        attn_in_grad = lax.dot_general(
            projected_grad,
            gathered[0].reshape(D, 3 * head_width),
            contract_cols,
            preferred_element_type=jnp.float32,
        )
        attn_back, mlp_back = (
            lax.psum_scatter(
                attn_in_grad.astype(jnp.bfloat16), "tensor", scatter_dimension=0, tiled=True
            ).astype(jnp.float32),
            lax.psum_scatter(
                mlp_in_grad.astype(jnp.bfloat16), "tensor", scatter_dimension=0, tiled=True
            ).astype(jnp.float32),
        )
        norm_back = jax.vjp(norm_pair, layer_in, norm_gains[layer_index], norm_shifts[layer_index])[
            1
        ]
        input_part, gain_part, shift_part = norm_back((attn_back, mlp_back))
        gain_terms[layer_index] = gain_part
        shift_terms[layer_index] = shift_part
        resid_grad = resid_grad + input_part
        weight_terms[layer_index] = (
            lax.psum_scatter(
                qkv_grad.astype(jnp.bfloat16), "dp", scatter_dimension=0, tiled=True
            ).astype(jnp.float32),
            lax.psum_scatter(
                out_grad.astype(jnp.bfloat16), "dp", scatter_dimension=0, tiled=True
            ).astype(jnp.float32),
            lax.psum_scatter(
                up_grad.astype(jnp.bfloat16), "dp", scatter_dimension=0, tiled=True
            ).astype(jnp.float32),
            lax.psum_scatter(
                down_grad.astype(jnp.bfloat16), "dp", scatter_dimension=0, tiled=True
            ).astype(jnp.float32),
        )
    qkv_stack = jnp.stack([weight_terms[layer_index][0] for layer_index in range(LAYERS)])
    out_stack = jnp.stack([weight_terms[layer_index][1] for layer_index in range(LAYERS)])
    up_stack = jnp.stack([weight_terms[layer_index][2] for layer_index in range(LAYERS)])
    down_stack = jnp.stack([weight_terms[layer_index][3] for layer_index in range(LAYERS)])
    bias_sums = lax.psum((jnp.stack(qkv_bias_terms), jnp.stack(up_bias_terms)), "dp")
    norm_sums = lax.psum(
        (jnp.stack(gain_terms), jnp.stack(shift_terms), jnp.stack(out_bias_terms)), ("dp", "tensor")
    )
    return (
        output,
        resid_grad,
        qkv_stack,
        bias_sums[0],
        out_stack,
        up_stack,
        bias_sums[1],
        down_stack,
        norm_sums[0],
        norm_sums[1],
        norm_sums[2],
    )


def solution(mesh):
    in_specs = (
        P(("dp", "tensor"), None),
        P(None, "dp", None, "tensor"),
        P(None, None, "tensor"),
        P(None, "dp", "tensor"),
        P(None, "dp", "tensor"),
        P(None, "tensor"),
        P(None, "dp", "tensor"),
        P(),
        P(),
        P(),
        P(("dp", "tensor"), None),
    )
    out_specs = (
        P(("dp", "tensor"), None),
        P(("dp", "tensor"), None),
        P(None, "dp", None, "tensor"),
        P(None, None, "tensor"),
        P(None, "dp", "tensor"),
        P(None, "dp", "tensor"),
        P(None, "tensor"),
        P(None, "dp", "tensor"),
        P(),
        P(),
        P(),
    )
    return jax.shard_map(local, mesh=mesh, in_specs=in_specs, out_specs=out_specs, check_vma=False)
```

profile of v0, /device:TPU:1, one launch (start us, length us, event | category | flops | bytes accessed | tf_op | source)
XLA Modules:
  0.0 1418.5 jit_solution(992630355511443120)
XLA Ops:
  17.2 42.1 %all-gather = bf16[1,1024,3,128]{3,1,2,0:T(8,128)(2,1)S(1)} all-gather(bf16[1,64,3,128]{3,1,2,0:T(8,128)(2,1)S(1)} %get-tuple-element.617), channel_id=2, replica_groups=mesh['dp'=16,'tensor'=8] {'dp'}, dimensions={1}, use_global_device_ids=true | all-gather | bytes 835584 | tf_op jit(solution)/shard_map/all_gather | solution.py:191
  59.6 20.7 %all-gather.1 = bf16[1,1024,128]{2,1,0:T(8,128)(2,1)S(1)} all-gather(bf16[1,64,128]{2,1,0:T(8,128)(2,1)S(1)} %get-tuple-element.627), channel_id=3, replica_groups=mesh['dp'=16,'tensor'=8] {'dp'}, dimensions={1}, use_global_device_ids=true | all-gather | bytes 278528 | tf_op jit(solution)/shard_map/all_gather | solution.py:192
  83.4 4.5 collective-permute-start
  88.0 20.6 %all-gather.31.cloned.1.call-done = bf16[1,1024,512]{2,1,0:T(8,128)(2,1)} async-done(((bf16[1,64,512]{2,1,0:T(8,128)(2,1)}), bf16[1,1024,512]{2,1,0:T(8,128)(2,1)}) %all-gather.31.cloned.1.call-update) | async-done | bytes 1048592 | tf_op jit(solution)/shard_map/all_gather | solution.py:193
  108.5 36.7 %all-gather.21.cloned.1.call-done = bf16[1024,1024]{1,0:T(8,128)(2,1)} async-done(((bf16[128,1024]{1,0:T(8,128)(2,1)}), bf16[1024,1024]{1,0:T(8,128)(2,1)}) %all-gather.21.cloned.1.call-update) | async-done | bytes 2097168 | tf_op jit(solution)/shard_map/all_gather | solution.py:199
  145.2 8.5 multiply_convert_fusion.3
  155.6 16.0 %while.56 = (s32[]{:T(128)}, bf16[2,512,2,64]{1,3,2,0:T(8,128)(2,1)S(1)}, f32[2,2,512]{2,1,0:T(2,128)S(1)}, s32[2,512]{1,0:T(2,128)S(1)}, bf16[2,512,2,64]{1,3,2...) while((s32[]{:T(128)}, ...), condition=%wide.region_5.6_spmd.clone, body=%wide.region_2.5_spmd.clone.sunk | while | flops 564139008 | bytes 30861428 | solution.py:74
  175.5 22.7 %all-gather.33.cloned.1.call-done = bf16[1,1024,512]{2,1,0:T(8,128)(2,1)} async-done(((bf16[1,64,512]{2,1,0:T(8,128)(2,1)}), bf16[1,1024,512]{2,1,0:T(8,128)(2,1)}) %all-gather.33.cloned.1.call-update) | async-done | bytes 1048592 | tf_op jit(solution)/shard_map/all_gather | solution.py:194
  198.1 5.1 add_convert_fusion.1
  205.3 33.9 %reduce-scatter.15.cloned.1.call-done = bf16[128,1024]{1,0:T(8,128)(2,1)} async-done(((bf16[1024,1024]{1,0:T(8,128)(2,1)}), bf16[128,1024]{1,0:T(8,128)(2,1)}) %reduce-scatter.15.cloned.1.call-update) | async-done | bytes 262160 | tf_op jit(solution)/shard_map/reduce_scatter | solution.py:222
  244.9 33.8 %all-gather.4 = bf16[1,1024,3,128]{3,1,2,0:T(8,128)(2,1)S(1)} all-gather(bf16[1,64,3,128]{3,1,2,0:T(8,128)(2,1)S(1)} %get-tuple-element.616), channel_id=6, replica_groups=mesh['dp'=16,'tensor'=8] {'dp'}, dimensions={1}, use_global_device_ids=true | all-gather | bytes 835584 | tf_op jit(solution)/shard_map/all_gather | solution.py:191
  279.0 20.4 %all-gather.5 = bf16[1,1024,128]{2,1,0:T(8,128)(2,1)S(1)} all-gather(bf16[1,64,128]{2,1,0:T(8,128)(2,1)S(1)} %get-tuple-element.626), channel_id=7, replica_groups=mesh['dp'=16,'tensor'=8] {'dp'}, dimensions={1}, use_global_device_ids=true | all-gather | bytes 278528 | tf_op jit(solution)/shard_map/all_gather | solution.py:192
  299.4 28.5 %all-gather.27.cloned.1.call-done = bf16[1024,1024]{1,0:T(8,128)(2,1)} async-done(((bf16[128,1024]{1,0:T(8,128)(2,1)}), bf16[1024,1024]{1,0:T(8,128)(2,1)}) %all-gather.27.cloned.1.call-update) | async-done | bytes 2097168 | tf_op jit(solution)/shard_map/all_gather | solution.py:274
  334.1 36.8 %all-gather.23.cloned.1.call-done = bf16[1024,1024]{1,0:T(8,128)(2,1)} async-done(((bf16[128,1024]{1,0:T(8,128)(2,1)}), bf16[1024,1024]{1,0:T(8,128)(2,1)}) %all-gather.23.cloned.1.call-update) | async-done | bytes 2097168 | tf_op jit(solution)/shard_map/all_gather | solution.py:198
  373.9 10.0 collective-permute-start.1
  383.8 40.1 %all-gather.35.cloned.1.call-done = bf16[1,1024,512]{2,1,0:T(8,128)(2,1)} async-done(((bf16[1,64,512]{2,1,0:T(8,128)(2,1)}), bf16[1,1024,512]{2,1,0:T(8,128)(2,1)}) %all-gather.35.cloned.1.call-update) | async-done | bytes 1048592 | tf_op jit(solution)/shard_map/all_gather | solution.py:193
  423.9 36.5 %all-gather.25.cloned.1.call-done = bf16[1024,1024]{1,0:T(8,128)(2,1)} async-done(((bf16[128,1024]{1,0:T(8,128)(2,1)}), bf16[1024,1024]{1,0:T(8,128)(2,1)}) %all-gather.25.cloned.1.call-update) | async-done | bytes 2097168 | tf_op jit(solution)/shard_map/all_gather | solution.py:199
  460.4 10.0 convert_reduce_fusion
  471.0 4.2 convolution_convert_fusion.3
  476.6 16.0 %while.57 = (s32[]{:T(128)}, bf16[2,512,2,64]{1,3,2,0:T(8,128)(2,1)S(1)}, f32[2,2,512]{2,1,0:T(2,128)S(1)}, s32[2,512]{1,0:T(2,128)S(1)}, bf16[2,512,2,64]{1,3,2...) while((s32[]{:T(128)}, ...), condition=%wide.region_12.13_spmd.clone, body=%wide.region_9.12_spmd.clone.sunk | while | flops 564139008 | bytes 30861428 | solution.py:74
  493.5 51.4 %while.58 = (s32[]{:T(128)}, f32[2048,2,64]{0,2,1:T(8,128)S(1)}, f32[2048,2,64]{0,2,1:T(8,128)}, f32[2,512,2,64]{1,0,3,2:T(2,128)}, bf16[2,512,2,64]{1,3,2,0:T(8...) while((s32[]{:T(128)}, f32[2048,2,64]{0,2,1:T(8,128)S(1)}, ...), condition=%wide.region_17.18_spmd.clone, body=%wide.region_15.17_spmd.clone.sunk | while | flops 1377113088 | bytes 161799504 | solution.py:122
  504.1 5.8 dynamic_update_slice.40
  514.7 4.6 fusion.306
  529.6 5.8 dynamic_update_slice.40
  540.1 4.9 fusion.306
  547.0 8.0 collective-permute-start.2
  555.5 8.6 collective-permute-done.2
  578.9 27.5 %reduce-scatter.21.cloned.1.call-done = bf16[128,1024]{1,0:T(8,128)(2,1)} async-done(((bf16[1024,1024]{1,0:T(8,128)(2,1)}), bf16[128,1024]{1,0:T(8,128)(2,1)}) %reduce-scatter.21.cloned.1.call-update) | async-done | bytes 262160 | tf_op jit(solution)/shard_map/reduce_scatter | solution.py:335
  608.5 41.8 %reduce-scatter.17.cloned.1.call-done = bf16[128,1024]{1,0:T(8,128)(2,1)} async-done(((bf16[1024,1024]{1,0:T(8,128)(2,1)}), bf16[128,1024]{1,0:T(8,128)(2,1)}) %reduce-scatter.17.cloned.1.call-update) | async-done | bytes 262160 | tf_op jit(solution)/shard_map/reduce_scatter | solution.py:222
  656.5 38.3 %all-gather.29.cloned.1.call-done = bf16[1024,1024]{1,0:T(8,128)(2,1)} async-done(((bf16[128,1024]{1,0:T(8,128)(2,1)}), bf16[1024,1024]{1,0:T(8,128)(2,1)}) %all-gather.29.cloned.1.call-update) | async-done | bytes 2097168 | tf_op jit(solution)/shard_map/all_gather | solution.py:274
  723.8 53.3 %while.59 = (s32[]{:T(128)}, f32[2048,2,64]{0,2,1:T(8,128)S(1)}, f32[2048,2,64]{0,2,1:T(8,128)}, f32[2,512,2,64]{1,0,3,2:T(2,128)}, bf16[2,512,2,64]{1,3,2,0:T(8...) while((s32[]{:T(128)}, f32[2048,2,64]{0,2,1:T(8,128)S(1)}, ...), condition=%wide.region_24.25_spmd.clone, body=%wide.region_22.24_spmd.clone.sunk | while | flops 1377113088 | bytes 161800000 | solution.py:122
  735.1 5.8 dynamic_update_slice.41
  745.6 4.7 fusion.319
  761.6 5.8 dynamic_update_slice.41
  772.1 5.1 fusion.319
  779.1 7.9 collective-permute-start.3
  791.5 4.7 collective-permute-done.3
  808.8 26.1 %reduce-scatter.31.cloned.1.call-done = bf16[64,128]{1,0:T(8,128)(2,1)} async-done(((bf16[1024,128]{1,0:T(8,128)(2,1)}), bf16[64,128]{1,0:T(8,128)(2,1)}) %reduce-scatter.31.cloned.1.call-update) | async-done | bytes 16400 | tf_op jit(solution)/shard_map/reduce_scatter | solution.py:353
  836.4 35.9 %all-reduce.25 = (f32[2,3,128]{2,1,0:T(4,128)S(1)}, f32[2,512]{1,0:T(2,128)}) all-reduce(f32[2,3,128]{2,1,0:T(4,128)S(1)} %pad_maximum_fusion.12, f32[2,512]{1,0:T(2,128)S(1)} %pad_maximum_fusion.13), channel_id=1, replica_groups=mesh['dp'=16,'tensor'=8] {'dp'}, use_global_device_ids=true, to_apply=%region_32.33 | all-reduce | flops 1792 | bytes 14336 | tf_op jit(solution)/shard_map/psum | solution.py:367
  872.9 31.7 %reduce-scatter.41.cloned.1.call-done = bf16[64,512]{1,0:T(8,128)(2,1)} async-done(((bf16[1024,512]{1,0:T(8,128)(2,1)}), bf16[64,512]{1,0:T(8,128)(2,1)}) %reduce-scatter.41.cloned.1.call-update) | async-done | bytes 65552 | tf_op jit(solution)/shard_map/reduce_scatter | solution.py:359
  904.6 70.1 %reduce-scatter.39.cloned.1.call-done = bf16[64,512]{1,0:T(8,128)(2,1)} async-done(((bf16[1024,512]{1,0:T(8,128)(2,1)}), bf16[64,512]{1,0:T(8,128)(2,1)}) %reduce-scatter.39.cloned.1.call-update) | async-done | bytes 65552 | tf_op jit(solution)/shard_map/reduce_scatter | solution.py:359
  976.3 68.2 %reduce-scatter.37.cloned.1.call-done = bf16[64,512]{1,0:T(8,128)(2,1)} async-done(((bf16[1024,512]{1,0:T(8,128)(2,1)}), bf16[64,512]{1,0:T(8,128)(2,1)}) %reduce-scatter.37.cloned.1.call-update) | async-done | bytes 65552 | tf_op jit(solution)/shard_map/reduce_scatter | solution.py:356
  1044.4 70.1 %reduce-scatter.35.cloned.1.call-done = bf16[64,512]{1,0:T(8,128)(2,1)} async-done(((bf16[1024,512]{1,0:T(8,128)(2,1)}), bf16[64,512]{1,0:T(8,128)(2,1)}) %reduce-scatter.35.cloned.1.call-update) | async-done | bytes 65552 | tf_op jit(solution)/shard_map/reduce_scatter | solution.py:356
  1116.1 67.3 %reduce-scatter.29.cloned.1.call-done = bf16[64,3,128]{2,0,1:T(8,128)(2,1)} async-done(((bf16[1024,3,128]{2,0,1:T(8,128)(2,1)}), bf16[64,3,128]{2,0,1:T(8,128)(2,1)}) %reduce-scatter.29.cloned.1.call-update) | async-done | bytes 49168 | tf_op jit(solution)/shard_map/reduce_scatter | solution.py:350
  1183.4 69.4 %reduce-scatter.27.cloned.1.call-done = bf16[64,3,128]{2,0,1:T(8,128)(2,1)} async-done(((bf16[1024,3,128]{2,0,1:T(8,128)(2,1)}), bf16[64,3,128]{2,0,1:T(8,128)(2,1)}) %reduce-scatter.27.cloned.1.call-update) | async-done | bytes 49168 | tf_op jit(solution)/shard_map/reduce_scatter | solution.py:350
  1254.4 39.1 %reduce-scatter.23.cloned.1.call-done = bf16[128,1024]{1,0:T(8,128)(2,1)} async-done(((bf16[1024,1024]{1,0:T(8,128)(2,1)}), bf16[128,1024]{1,0:T(8,128)(2,1)}) %reduce-scatter.23.cloned.1.call-update) | async-done | bytes 262160 | tf_op jit(solution)/shard_map/reduce_scatter | solution.py:338
  1293.5 43.6 %reduce-scatter.25.cloned.1.call-done = bf16[128,1024]{1,0:T(8,128)(2,1)} async-done(((bf16[1024,1024]{1,0:T(8,128)(2,1)}), bf16[128,1024]{1,0:T(8,128)(2,1)}) %reduce-scatter.25.cloned.1.call-update) | async-done | bytes 262160 | tf_op jit(solution)/shard_map/reduce_scatter | solution.py:335
  1339.9 69.3 %all-reduce.24 = (f32[2,2,1024]{2,1,0:T(2,128)}, f32[2,2,1024]{2,1,0:T(2,128)}, f32[2,1024]{1,0:T(2,128)}) all-reduce(f32[2,2,1024]{2,1,0:T(2,128)S(1)} %pad_maximum_fusion.9, f32[2,2,1024]{2,1,0:T(2,128)S(1)} %pad_maximum_fusion.10, f32[2,1024]{1,0:T(2,128)S(1)} %pad_maximum_fusion.11), channel_id=1, replica_groups=mesh['dp'=16,'tensor'=8] {'dp','tensor'}, use_global_device_ids=true, to_apply=%region_46.47 | all-reduce | flops 10240 | bytes 81920 | tf_op jit(solution)/shard_map/psum | solution.py:368
  (513 shorter events, 216.7 us)
Async XLA Ops:
  7.2 73.2 %all-gather.19.cloned.1.call-start = ((), (), s32[]{:S(2)}) async-start(), calls=%async_computation.14 | async-start | bytes 2359296 | tf_op jit(solution)/shard_map/all_gather | solution.py:198
  10.9 230.6 %copy-start.66 = (f32[1,1,1024]{2,1,0:T(1,128)}, f32[1,1,1024]{2,1,0:T(1,128)S(1)}, u32[]{:S(2)}) copy-start(f32[1,1,1024]{2,1,0:T(1,128)S(1)} %get-tuple-element.630) | copy-start | bytes 12292
  10.9 230.6 %copy-start.68 = (f32[1,1,1024]{2,1,0:T(1,128)}, f32[1,1,1024]{2,1,0:T(1,128)S(1)}, u32[]{:S(2)}) copy-start(f32[1,1,1024]{2,1,0:T(1,128)S(1)} %get-tuple-element.633) | copy-start | bytes 12292
  13.7 66.6 %copy-start.89 = (bf16[2,512]{1,0:T(2,128)(2,1)S(1)}, bf16[2,512]{1,0:T(2,128)(2,1)}, u32[]{:S(2)}) copy-start(bf16[2,512]{1,0:T(2,128)(2,1)} %param.24) | copy-start | bytes 6148
  13.7 94.8 %all-gather.31.cloned.1.call-start = ((), (), s32[]{:S(2)}) async-start(), calls=%async_computation.34 | async-start | bytes 1114112 | tf_op jit(solution)/shard_map/all_gather | solution.py:193
  15.3 129.9 %all-gather.21.cloned.1.call-start = ((), (), s32[]{:S(2)}) async-start(), calls=%async_computation.15 | async-start | bytes 2359296 | tf_op jit(solution)/shard_map/all_gather | solution.py:199
  16.1 182.1 %all-gather.33.cloned.1.call-start = ((), (), s32[]{:S(2)}) async-start(), calls=%async_computation.35 | async-start | bytes 1114112 | tf_op jit(solution)/shard_map/all_gather | solution.py:194
  16.8 222.4 %reduce-scatter.15.cloned.1.call-start = ((), (), s32[]{:S(2)}) async-start(), calls=%async_computation.16 | async-start | bytes 2359296 | tf_op jit(solution)/shard_map/reduce_scatter | solution.py:222
  17.2 356.5 %copy-start.40 = (f32[1024,16]{0,1:T(8,128)}, f32[1024,16]{0,1:T(8,128)S(1)}, u32[]{:S(2)}) copy-start(f32[1024,16]{0,1:T(8,128)S(1)} %get-tuple-element.629) | copy-start | bytes 196612
  17.2 356.5 %copy-start.42 = (f32[1024,16]{0,1:T(8,128)}, f32[1024,16]{0,1:T(8,128)S(1)}, u32[]{:S(2)}) copy-start(f32[1024,16]{0,1:T(8,128)S(1)} %get-tuple-element.628) | copy-start | bytes 196612
  80.4 91.6 %copy-start.28 = (bf16[1,1024,128]{2,1,0:T(8,128)(2,1)}, bf16[1,1024,128]{2,1,0:T(8,128)(2,1)S(1)}, u32[]{:S(2)}) copy-start(bf16[1,1024,128]{2,1,0:T(8,128)(2,1)S(1)} %all-gather.1) | copy-start | bytes 786436
  80.4 380.1 %copy-start.86 = (f32[1,512]{1,0:T(1,128)}, f32[1,512]{1,0:T(1,128)S(1)}, u32[]{:S(2)}) copy-start(f32[1,512]{1,0:T(1,128)S(1)} %get-tuple-element.640) | copy-start | bytes 6148
  83.4 70.9 %collective-permute-start = (bf16[2,1024,128]{1,2,0:T(8,128)(2,1)S(1)}, bf16[2,1024,128]{1,2,0:T(8,128)(2,1)}, u32[]{:S(2)}, u32[]{:S(2)}) collective-permute-start(bf16[2,1024,128]{1,2,0:T(8,128)(2,1)S(1)} %pad_maximum_fusion.2), channel_id=1, source_target_pairs={{0,8},{8,16},{16,24},{24,32},{32,40},{40,48},{48,56},{56,64},{64,7... | collective-permute-start | bytes 1572872 | tf_op jit(solution)/shard_map/ppermute | solution.py:22
  203.3 96.1 %all-gather.37.cloned.1.call-start = ((), (), s32[]{:S(2)}) async-start(), calls=%async_computation.37 | async-start | bytes 1114112 | tf_op jit(solution)/shard_map/all_gather | solution.py:194
  203.9 124.0 %all-gather.27.cloned.1.call-start = ((), (), s32[]{:S(2)}) async-start(), calls=%async_computation.20 | async-start | bytes 2359296 | tf_op jit(solution)/shard_map/all_gather | solution.py:274
  204.6 166.2 %all-gather.23.cloned.1.call-start = ((), (), s32[]{:S(2)}) async-start(), calls=%async_computation.17 | async-start | bytes 2359296 | tf_op jit(solution)/shard_map/all_gather | solution.py:198
  205.3 73.7 %copy-start.56 = (f32[1,1024]{1,0:T(1,128)}, f32[1,1024]{1,0:T(1,128)S(1)}, u32[]{:S(2)}) copy-start(f32[1,1024]{1,0:T(1,128)S(1)} %get-tuple-element.639) | copy-start | bytes 12292
  243.5 180.4 %all-gather.35.cloned.1.call-start = ((), (), s32[]{:S(2)}) async-start(), calls=%async_computation.36 | async-start | bytes 1114112 | tf_op jit(solution)/shard_map/all_gather | solution.py:193
  244.2 216.2 %all-gather.25.cloned.1.call-start = ((), (), s32[]{:S(2)}) async-start(), calls=%async_computation.18 | async-start | bytes 2359296 | tf_op jit(solution)/shard_map/all_gather | solution.py:199
  244.8 334.0 %reduce-scatter.19.cloned.1.call-start = ((), (), s32[]{:S(2)}) async-start(), calls=%async_computation.21 | async-start | bytes 2359296 | tf_op jit(solution)/shard_map/reduce_scatter | solution.py:338
  279.0 91.9 %copy-start.52 = (bf16[1,1024,3,128]{1,3,2,0:T(8,128)(2,1)}, bf16[1,1024,3,128]{1,3,2,0:T(8,128)(2,1)S(1)}, u32[]{:S(2)}) copy-start(bf16[1,1024,3,128]{1,3,2,0:T(8,128)(2,1)S(1)} %copy.50) | copy-start | bytes 2359300
  373.9 101.5 %collective-permute-start.1 = (bf16[2,1024,128]{1,2,0:T(8,128)(2,1)S(1)}, bf16[2,1024,128]{1,2,0:T(8,128)(2,1)}, u32[]{:S(2)}, u32[]{:S(2)}) collective-permute-start(bf16[2,1024,128]{1,2,0:T(8,128)(2,1)S(1)} %pad_maximum_fusion.3), channel_id=1, source_target_pairs={{0,8},{8,16},{16,24},{24,32},{32,40},{40,48},{48,56},{56,64},{64,7... | collective-permute-start | bytes 1572872 | tf_op jit(solution)/shard_map/ppermute | solution.py:22
  475.3 131.1 %reduce-scatter.21.cloned.1.call-start = ((), (), s32[]{:S(2)}) async-start(), calls=%async_computation.22 | async-start | bytes 2359296 | tf_op jit(solution)/shard_map/reduce_scatter | solution.py:335
  547.0 17.1 %collective-permute-start.2 = (bf16[2,1024,128]{1,2,0:T(8,128)(2,1)}, bf16[2,1024,128]{1,2,0:T(8,128)(2,1)}, u32[]{:S(2)}, u32[]{:S(2)}) collective-permute-start(bf16[2,1024,128]{1,2,0:T(8,128)(2,1)} %fusion.131), channel_id=1, source_target_pairs={{8,0},{16,8},{24,16},{32,24},{40,32},{48,40},{56,48},{64,56},{72,6... | collective-permute-start | bytes 1572872 | tf_op jit(solution)/shard_map/ppermute | solution.py:22
  570.7 79.6 %reduce-scatter.17.cloned.1.call-start = ((), (), s32[]{:S(2)}) async-start(), calls=%async_computation.19 | async-start | bytes 2359296 | tf_op jit(solution)/shard_map/reduce_scatter | solution.py:222
  578.7 71.6 %copy-start.71 = (f32[1,1024]{1,0:T(1,128)S(1)}, f32[1,1024]{1,0:T(1,128)}, u32[]{:S(2)}) copy-start(f32[1,1024]{1,0:T(1,128)} %get-tuple-element.638) | copy-start | bytes 12292
  578.8 74.5 %copy-start.33 = (bf16[128,1024]{1,0:T(8,128)(2,1)S(1)}, bf16[128,1024]{1,0:T(8,128)(2,1)}, u32[]{:S(2)}) copy-start(bf16[128,1024]{1,0:T(8,128)(2,1)} %param.29) | copy-start | bytes 786436
  578.8 76.0 %copy-start.18 = (bf16[1024,1024]{1,0:T(8,128)(2,1)S(1)}, bf16[1024,1024]{1,0:T(8,128)(2,1)}, u32[]{:S(2)}) copy-start(bf16[1024,1024]{1,0:T(8,128)(2,1)} %all-gather.27.cloned.1.call-done) | copy-start | bytes 6291460
  578.8 116.0 %all-gather.29.cloned.1.call-start = ((), (), s32[]{:S(2)}) async-start(), calls=%async_computation.23 | async-start | bytes 2359296 | tf_op jit(solution)/shard_map/all_gather | solution.py:274
  654.7 154.1 %reduce-scatter.33.cloned.1.call-start = ((), (), s32[]{:S(2)}) async-start(), calls=%async_computation.29 | async-start | bytes 278528 | tf_op jit(solution)/shard_map/reduce_scatter | solution.py:353
  656.5 178.5 %reduce-scatter.31.cloned.1.call-start = ((), (), s32[]{:S(2)}) async-start(), calls=%async_computation.28 | async-start | bytes 278528 | tf_op jit(solution)/shard_map/reduce_scatter | solution.py:353
  697.9 206.7 %reduce-scatter.41.cloned.1.call-start = ((), (), s32[]{:S(2)}) async-start(), calls=%async_computation.33 | async-start | bytes 1114112 | tf_op jit(solution)/shard_map/reduce_scatter | solution.py:359
  702.0 272.7 %reduce-scatter.39.cloned.1.call-start = ((), (), s32[]{:S(2)}) async-start(), calls=%async_computation.32 | async-start | bytes 1114112 | tf_op jit(solution)/shard_map/reduce_scatter | solution.py:359
  705.7 338.7 %reduce-scatter.37.cloned.1.call-start = ((), (), s32[]{:S(2)}) async-start(), calls=%async_computation.31 | async-start | bytes 1114112 | tf_op jit(solution)/shard_map/reduce_scatter | solution.py:356
  709.6 404.9 %reduce-scatter.35.cloned.1.call-start = ((), (), s32[]{:S(2)}) async-start(), calls=%async_computation.30 | async-start | bytes 1114112 | tf_op jit(solution)/shard_map/reduce_scatter | solution.py:356
  722.6 460.8 %reduce-scatter.29.cloned.1.call-start = ((), (), s32[]{:S(2)}) async-start(), calls=%async_computation.27 | async-start | bytes 835584 | tf_op jit(solution)/shard_map/reduce_scatter | solution.py:350
  779.1 17.1 %collective-permute-start.3 = (bf16[2,1024,128]{1,2,0:T(8,128)(2,1)}, bf16[2,1024,128]{1,2,0:T(8,128)(2,1)}, u32[]{:S(2)}, u32[]{:S(2)}) collective-permute-start(bf16[2,1024,128]{1,2,0:T(8,128)(2,1)} %fusion.130), channel_id=1, source_target_pairs={{8,0},{16,8},{24,16},{32,24},{40,32},{48,40},{56,48},{64,56},{72,6... | collective-permute-start | bytes 1572872 | tf_op jit(solution)/shard_map/ppermute | solution.py:22
  791.0 461.9 %reduce-scatter.27.cloned.1.call-start = ((), (), s32[]{:S(2)}) async-start(), calls=%async_computation.26 | async-start | bytes 835584 | tf_op jit(solution)/shard_map/reduce_scatter | solution.py:350
  801.5 492.0 %reduce-scatter.23.cloned.1.call-start = ((), (), s32[]{:S(2)}) async-start(), calls=%async_computation.24 | async-start | bytes 2359296 | tf_op jit(solution)/shard_map/reduce_scatter | solution.py:338
  804.1 532.9 %reduce-scatter.25.cloned.1.call-start = ((), (), s32[]{:S(2)}) async-start(), calls=%async_computation.25 | async-start | bytes 2359296 | tf_op jit(solution)/shard_map/reduce_scatter | solution.py:335
  808.0 529.1 %copy-start.60 = (f32[1,1,1024]{2,1,0:T(1,128)S(1)}, f32[1,1,1024]{2,1,0:T(1,128)}, u32[]{:S(2)}) copy-start(f32[1,1,1024]{2,1,0:T(1,128)} %copy-done.59) | copy-start | bytes 12292
  808.0 529.1 %copy-start.62 = (f32[1,1,1024]{2,1,0:T(1,128)S(1)}, f32[1,1,1024]{2,1,0:T(1,128)}, u32[]{:S(2)}) copy-start(f32[1,1,1024]{2,1,0:T(1,128)} %copy-done.61) | copy-start | bytes 12292
  808.0 529.0 %copy-start.80 = (f32[128]{0:T(128)S(1)}, f32[128]{0:T(128)}, u32[]{:S(2)}) copy-start(f32[128]{0:T(128)} %copy-done.79) | copy-start | bytes 1540
  808.0 530.3 %copy-start.99 = (f32[128]{0:T(128)S(1)}, f32[128]{0:T(128)}, u32[]{:S(2)}) copy-start(f32[128]{0:T(128)} %copy-done.98) | copy-start | bytes 1540
  808.0 530.4 %copy-start.94 = (f32[128]{0:T(128)S(1)}, f32[128]{0:T(128)}, u32[]{:S(2)}) copy-start(f32[128]{0:T(128)} %copy-done.93) | copy-start | bytes 1540
  808.0 601.2 %copy-start.21 = (f32[128,1024]{1,0:T(8,128)S(1)}, f32[128,1024]{1,0:T(8,128)}, u32[]{:S(2)}) copy-start(f32[128,1024]{1,0:T(8,128)} %copy-done.20) | copy-start | bytes 1572868
  808.0 601.2 %copy-start.34 = (bf16[128,1024]{1,0:T(8,128)(2,1)S(1)}, bf16[128,1024]{1,0:T(8,128)(2,1)}, u32[]{:S(2)}) copy-start(bf16[128,1024]{1,0:T(8,128)(2,1)} %param.29) | copy-start | bytes 786436
  808.0 601.2 %copy-start.97 = (f32[128]{0:T(128)S(1)}, f32[128]{0:T(128)}, u32[]{:S(2)}) copy-start(f32[128]{0:T(128)} %copy-done.96) | copy-start | bytes 1540
  (97 other events, 1112.6 us)
Sparse Core Ops, SparseCore 0:
  13.8 39.8 all-gather.18
  56.8 51.6 all-gather.30
  110.8 34.4 all-gather.20
  148.1 49.9 all-gather.32
  203.4 35.7 reduce-scatter.14
  242.1 49.5 all-gather.36
  293.3 34.4 all-gather.26
  330.1 40.7 all-gather.22
  373.9 49.9 all-gather.34
  426.0 34.4 all-gather.24
  475.4 41.7 reduce-scatter.18
  570.8 35.4 reduce-scatter.20
  608.7 41.5 reduce-scatter.16
  654.8 39.9 all-gather.28
  698.9 67.9 reduce-scatter.32
  770.4 64.5 reduce-scatter.30
  838.6 65.9 reduce-scatter.40
  908.7 65.9 reduce-scatter.38
  978.4 65.9 reduce-scatter.36
  1048.5 65.9 reduce-scatter.34
  1118.3 65.0 reduce-scatter.28
  1187.7 65.1 reduce-scatter.26
  1255.3 38.1 reduce-scatter.22
  1295.7 41.2 reduce-scatter.24
where the time goes:
time: 1420 us
  waiting for transfers between devices  866 us (61%)
  blocking collectives  222 us (16%)
  matrix products  158 us (11%)
  other arithmetic  67.3 us (5%)
  local copies, waits for them, and re-layouts  57.2 us (4%)
  starting transfers between devices  31.5 us (2%)
  between operations  16.3 us (1%)
    reduce_scatter x2, waiting for transfers between devices, local(): lax.psum_scatter(up_grad.astype(jnp.bfloat16), 'dp', scatter_dimension=0,...  138 us
    reduce_scatter x2, waiting for transfers between devices, local(): lax.psum_scatter(qkv_grad.astype(jnp.bfloat16), 'dp', scatter_dimension=0...  137 us
    reduce_scatter x2, waiting for transfers between devices, local(): lax.psum_scatter(down_grad.astype(jnp.bfloat16), 'dp', scatter_dimension=...  102 us
    all_gather x2, blocking collectives, local(): lax.all_gather(qkv_weight[layer_index], 'dp', axis=0, tiled=True)  75.9 us
    reduce_scatter x2, waiting for transfers between devices, local(): lax.psum_scatter(branch_rows(attended, activated, gathered[1], gathered[3...  75.7 us
    all_gather x2, waiting for transfers between devices, local(): lax.all_gather(mlp_in.astype(jnp.bfloat16), 'tensor', axis=0, tiled=True)  73.3 us
    reduce_scatter x2, waiting for transfers between devices, local(): lax.psum_scatter(attn_in_grad.astype(jnp.bfloat16), 'tensor', scatter_dim...  71 us
    psum x1, blocking collectives, local(): lax.psum((jnp.stack(gain_terms), jnp.stack(shift_terms), jnp.stack(out_bi...  69.3 us
  transfers between devices with their start and end apart: 28, of which 22 were waited for; matrix products, arithmetic and copies ran while one was open for 17% of the time, Pallas kernels for 0%

commit v1 on v0

v1 whole, which is shorter than its diff:
```python
import functools

import jax
import jax.numpy as jnp
from jax import lax
from jax.experimental import pallas as pl
from jax.experimental.pallas import tpu as pltpu
from jax.sharding import PartitionSpec as P

BF = jnp.bfloat16
F32 = jnp.float32
D = 1024
HD = 64
ROT = 16
LAYERS = 2
ROWS = 1024
QB = 256
EPS = 1e-05
MASKED = -1e30
SCALE = HD ** (-0.5)
VM = pl.BlockSpec(memory_space=pltpu.VMEM)
DMA = pltpu.SemaphoreType.DMA
NN = (((1,), (0,)), ((), ()))
NT = (((1,), (1,)), ((), ()))
TN = (((0,), (0,)), ((), ()))


def dot(a, b, dims=NN):
    return lax.dot_general(a, b, dims, preferred_element_type=F32)


def remote(src, dst, send, recv, dp, tensor):
    return pltpu.make_async_remote_copy(
        src_ref=src,
        dst_ref=dst,
        send_sem=send,
        recv_sem=recv,
        device_id=(dp, tensor),
        device_id_type=pl.DeviceIdType.MESH,
    )


def greet(peers):
    sem = pltpu.get_barrier_semaphore()
    for peer in peers:
        pl.semaphore_signal(sem, inc=1, device_id=peer, device_id_type=pl.DeviceIdType.MESH)
    pl.semaphore_wait(sem, len(peers))


def call(kernel, name, cid, out, scratch, *args):
    many = isinstance(out, (list, tuple))
    return pl.pallas_call(
        kernel,
        name=name,
        out_shape=out,
        in_specs=[VM] * len(args),
        out_specs=[VM] * len(out) if many else VM,
        scratch_shapes=scratch,
        compiler_params=pltpu.CompilerParams(
            collective_id=cid, has_side_effects=cid is not None, vmem_limit_bytes=56 << 20
        ),
    )(*args)


def sds(shape, dtype):
    return jax.ShapeDtypeStruct(shape, dtype)


def rows_gather_kernel(x_ref, o_ref, ss, rs):
    dp, t = lax.axis_index("dp"), lax.axis_index("tensor")
    x, y = t % 4, t // 4
    right, left, across = y * 4 + (x + 1) % 4, y * 4 + (x + 3) % 4, (1 - y) * 4 + x
    a_right, a_left = (1 - y) * 4 + (x + 1) % 4, (1 - y) * 4 + (x + 3) % 4
    greet([(dp, right), (dp, left), (dp, across)])
    half = x_ref.shape[0] // 2

    def make(i, src, dst, to):
        return remote(src, dst, ss.at[i], rs.at[i], dp, to)

    def top(slot):
        return o_ref.at[slot, 0:half]

    def bottom(slot):
        return o_ref.at[slot, half : 2 * half]

    c_across = make(0, x_ref, o_ref.at[t], across)
    c_right = make(1, x_ref, o_ref.at[t], right)
    c_left = make(2, x_ref, o_ref.at[t], left)
    c_across.start()
    c_right.start()
    c_left.start()
    o_ref[t] = x_ref[...]
    c_across.wait_recv()
    d_right = make(3, o_ref.at[across], o_ref.at[across], right)
    d_left = make(4, o_ref.at[across], o_ref.at[across], left)
    d_right.start()
    d_left.start()
    c_right.wait_recv()
    e_right = make(5, top(left), top(left), right)
    e_right.start()
    c_left.wait_recv()
    e_left = make(6, bottom(right), bottom(right), left)
    e_left.start()
    d_right.wait_recv()
    f_right = make(7, top(a_left), top(a_left), right)
    f_right.start()
    d_left.wait_recv()
    f_left = make(8, bottom(a_right), bottom(a_right), left)
    f_left.start()
    for c in (e_right, e_left, f_right, f_left):
        c.wait_recv()
    for c in (c_across, c_right, c_left, d_right, d_left, e_right, e_left, f_right, f_left):
        c.wait_send()


def rows_gather(x, cid):
    out = call(
        rows_gather_kernel, "rows_gather", cid, sds((8,) + x.shape, x.dtype), [DMA((9,)), DMA((9,))], x
    )
    return out.reshape(8 * x.shape[0], x.shape[1])


def rows_scatter_kernel(x_ref, o_ref, buf, ss, rs):
    dp, t = lax.axis_index("dp"), lax.axis_index("tensor")
    peers = [(dp, (t + d) % 8) for d in range(1, 8)]
    greet(peers)
    copies = []
    for i, (_, to) in enumerate(peers):
        c = remote(x_ref.at[to], buf.at[i], ss.at[i], rs.at[i], dp, to)
        c.start()
        copies.append(c)
    total = x_ref[t].astype(F32)
    for i, c in enumerate(copies):
        c.wait_recv()
        total = total + buf[i].astype(F32)
    o_ref[...] = total
    for c in copies:
        c.wait_send()


def rows_scatter(x, cid):
    x = x.reshape(8, x.shape[0] // 8, x.shape[1])
    return call(
        rows_scatter_kernel,
        "rows_scatter",
        cid,
        sds(x.shape[1:], F32),
        [pltpu.VMEM((7,) + x.shape[1:], x.dtype), DMA((7,)), DMA((7,))],
        x,
    )


def weights_gather_kernel(x_ref, o_ref, ss, rs):
    dp, t = lax.axis_index("dp"), lax.axis_index("tensor")
    z, yh, core = dp // 4, (dp // 2) % 2, dp % 2
    sibling = dp + 1 - 2 * core
    across = z * 4 + (1 - yh) * 2 + core
    steps = (1, 3, 2)
    ring = [((z + d) % 4) * 4 + yh * 2 + core for d in steps]
    greet([(sibling, t), (across, t)] + [(q, t) for q in ring])
    copies = []

    def send(slot, to, src=None):
        i = len(copies)
        c = remote(o_ref.at[slot] if src is None else src, o_ref.at[slot], ss.at[i], rs.at[i], to, t)
        c.start()
        copies.append(c)
        return c

    c_across = send(dp, across, x_ref)
    c_ring = [send(dp, q, x_ref) for q in ring]
    last = [send(dp, sibling, x_ref)]
    o_ref[dp] = x_ref[...]
    c_across.wait_recv()
    d_ring = [send(across, q) for q in ring]
    last.append(send(across, sibling))
    for y_part, group in ((yh, c_ring), (1 - yh, d_ring)):
        for c, d in zip(group, steps):
            c.wait_recv()
            last.append(send(((z + 4 - d) % 4) * 4 + y_part * 2 + core, sibling))
    for c in last:
        c.wait_recv()
    for c in copies:
        c.wait_send()


def weights_gather(x, cid):
    out = call(
        weights_gather_kernel,
        "weights_gather",
        cid,
        sds((16,) + x.shape, x.dtype),
        [DMA((15,)), DMA((15,))],
        x,
    )
    return out.reshape(16 * x.shape[0], x.shape[1])


CHIPS = sorted(
    [(dz, dy) for dz in range(4) for dy in range(2) if dz or dy],
    key=lambda c: -(min(c[0], 4 - c[0]) + 2 * c[1]),
)


def weights_scatter_kernel(x_ref, o_ref, pair, mid, buf, ss, rs):
    dp, t = lax.axis_index("dp"), lax.axis_index("tensor")
    z, yh, core = dp // 4, (dp // 2) % 2, dp % 2
    sibling = dp + 1 - 2 * core
    places = [((z + dz) % 4) * 4 + ((yh + dy) % 2) * 2 + core for dz, dy in CHIPS] + [dp]
    greet([(sibling, t)] + [(q, t) for q in places[:-1]])
    inner = []
    for i, place in enumerate(places):
        c = remote(x_ref.at[place + 1 - 2 * core], pair.at[i], ss.at[i], rs.at[i], sibling, t)
        c.start()
        inner.append(c)
    outer = []
    for i, place in enumerate(places):
        inner[i].wait_recv()
        both = x_ref[place].astype(F32) + pair[i].astype(F32)
        if i == 7:
            total = both
        else:
            mid[i] = both.astype(BF)
            c = remote(mid.at[i], buf.at[i], ss.at[8 + i], rs.at[8 + i], place, t)
            c.start()
            outer.append(c)
    for i, c in enumerate(outer):
        c.wait_recv()
        total = total + buf[i].astype(F32)
    o_ref[...] = total
    for c in inner + outer:
        c.wait_send()


def weights_scatter(x, cid):
    x = x.reshape(16, x.shape[0] // 16, x.shape[1])
    block = x.shape[1:]
    return call(
        weights_scatter_kernel,
        "weights_scatter",
        cid,
        sds(block, F32),
        [pltpu.VMEM((8,) + block, BF), pltpu.VMEM((7,) + block, BF), pltpu.VMEM((7,) + block, BF), DMA((15,)), DMA((15,))],
        x,
    )


def small_sums_kernel(every_ref, along_ref, every_out, along_out, first, mine, got, last, ss, rs):
    dp, t = lax.axis_index("dp"), lax.axis_index("tensor")
    group = [(dp, (t + d) % 8) for d in range(1, 8)]
    line = [((dp + d) % 16, t) for d in range(1, 16)]
    greet(group + line)
    depth = every_ref.shape[1]
    copies = []
    for i, (_, to) in enumerate(group):
        c = remote(every_ref.at[to], first.at[i], ss.at[i], rs.at[i], dp, to)
        c.start()
        copies.append(c)
    total = every_ref[t]
    for i in range(7):
        copies[i].wait_recv()
        total = total + first[i]
    mine[0:depth] = total
    mine[depth : depth + along_ref.shape[0]] = along_ref[...]
    for i, (to, _) in enumerate(line):
        c = remote(mine, got.at[dp], ss.at[7 + i], rs.at[7 + i], to, t)
        c.start()
        copies.append(c)
    got[dp] = mine[...]
    for c in copies[7:22]:
        c.wait_recv()
    total = got[0]
    for i in range(1, 16):
        total = total + got[i]
    along_out[...] = total[depth : depth + along_ref.shape[0]]
    last[...] = total[0:depth]
    for i, (_, to) in enumerate(group):
        c = remote(last, every_out.at[t], ss.at[22 + i], rs.at[22 + i], dp, to)
        c.start()
        copies.append(c)
    every_out[t] = last[...]
    for c in copies[22:]:
        c.wait_recv()
    for c in copies:
        c.wait_send()


def small_sums(every, along, cid):
    a, b = every.shape[1], along.shape[0]
    return call(
        small_sums_kernel,
        "small_sums",
        cid,
        [sds(every.shape, F32), sds(along.shape, F32)],
        [
            pltpu.VMEM((7, a, 128), F32),
            pltpu.VMEM((a + b, 128), F32),
            pltpu.VMEM((16, a + b, 128), F32),
            pltpu.VMEM((a, 128), F32),
            DMA((29,)),
            DMA((29,)),
        ],
        every,
        along,
    )


def head_mask(h):
    lane = lax.broadcasted_iota(jnp.int32, (1, 2 * HD), 1)
    return (lane // HD) == h


def only_head(value, h):
    return jnp.where(head_mask(h), value, jnp.zeros_like(value))


def transposed(value):
    return value.astype(F32).T.astype(value.dtype)


def causal_block():
    key = lax.broadcasted_iota(jnp.int32, (QB, QB), 0)
    query = lax.broadcasted_iota(jnp.int32, (QB, QB), 1)
    return query >= key


def attention_forward_kernel(q_ref, k_ref, v_ref, kp_ref, vp_ref, o_ref, lse_ref, o_t, v_t, vp_t):
    core = lax.axis_index("dp") % 2
    v_t[...] = transposed(v_ref[...])

    def block(j, earlier):
        cols = pl.ds(j * QB, QB)
        q_rows = q_ref[cols, :]
        for h in range(2):
            q_head = only_head(q_rows, h)
            heads = pl.ds(h * HD, HD)
            parts = []
            if earlier:
                parts += [(dot(kp_ref[pl.ds(i * 512, 512), :], q_head, NT), vp_t[heads, pl.ds(i * 512, 512)]) for i in range(2)]
            if j:
                parts.append((dot(k_ref[0 : j * QB, :], q_head, NT), v_t[heads, 0 : j * QB]))
            diagonal = jnp.where(causal_block(), dot(k_ref[cols, :], q_head, NT), MASKED)
            parts.append((diagonal, v_t[heads, cols]))
            top = functools.reduce(jnp.maximum, [jnp.max(s, axis=0, keepdims=True) for s, _ in parts])
            total, out = 0.0, 0.0
            for s, values in parts:
                weight = jnp.exp(s - top)
                total = total + jnp.sum(weight, axis=0, keepdims=True)
                out = out + dot(values, weight.astype(BF))
            o_t[heads, cols] = out / total
            lse_ref[h : h + 1, cols] = top + jnp.log(total)

    @pl.when(core == 1)
    def _():
        vp_t[...] = transposed(vp_ref[...])
        for j in range(ROWS // QB):
            block(j, True)

    @pl.when(core == 0)
    def _():
        for j in range(ROWS // QB):
            block(j, False)

    o_ref[...] = o_t[...].T.astype(BF)


def attention_forward(q, k, v, kp, vp):
    return call(
        attention_forward_kernel,
        "attention_forward",
        None,
        [sds((ROWS, 128), BF), sds((2, ROWS), F32)],
        [pltpu.VMEM((128, ROWS), F32), pltpu.VMEM((128, ROWS), BF), pltpu.VMEM((128, ROWS), BF)],
        q, k, v, kp, vp,
    )


def attention_backward_kernel(
    q_ref, k_ref, v_ref, kp_ref, vp_ref, lse_ref, o_ref, do_ref,
    dq_ref, dk_ref, dv_ref, dkp_ref, dvp_ref,
    dq_t, k_t, kp_t, delta, dkp_acc, dvp_acc,
):
    core = lax.axis_index("dp") % 2
    k_t[...] = transposed(k_ref[...])
    product = (do_ref[...].astype(F32) * o_ref[...].astype(F32)).T
    for h in range(2):
        delta[h : h + 1, :] = jnp.sum(product[h * HD : (h + 1) * HD], axis=0, keepdims=True)
    dq_t[...] = jnp.zeros_like(dq_t)
    dk_ref[...] = jnp.zeros_like(dk_ref)
    dv_ref[...] = jnp.zeros_like(dv_ref)

    def block(j, earlier):
        cols = pl.ds(j * QB, QB)
        q_rows, do_rows = q_ref[cols, :], do_ref[cols, :]
        q_heads = [only_head(q_rows, h) for h in range(2)]
        do_heads = [only_head(do_rows, h) for h in range(2)]
        q_both = jnp.concatenate(q_heads, axis=0)
        do_both = jnp.concatenate(do_heads, axis=0)

        def part(keys, values, turned, dk_acc, dv_acc, rows, masked):
            key_rows, value_rows = keys[rows, :], values[rows, :]
            probs, slopes = [], []
            for h in range(2):
                s = dot(key_rows, q_heads[h], NT)
                p = jnp.exp(s - lse_ref[h : h + 1, cols])
                if masked:
                    p = jnp.where(causal_block(), p, 0.0)
                dp = dot(value_rows, do_heads[h], NT)
                ds = (p * (dp - delta[h : h + 1, cols])).astype(BF)
                heads = pl.ds(h * HD, HD)
                dq_t[heads, cols] += dot(turned[heads, rows], ds)
                probs.append(p.astype(BF))
                slopes.append(ds)
            dv_acc[rows, :] += dot(jnp.concatenate(probs, axis=1), do_both)
            dk_acc[rows, :] += dot(jnp.concatenate(slopes, axis=1), q_both)

        if earlier:
            for i in range(ROWS // 512):
                part(kp_ref, vp_ref, kp_t, dkp_acc, dvp_acc, pl.ds(i * 512, 512), False)
        for i in range(j):
            part(k_ref, v_ref, k_t, dk_ref, dv_ref, pl.ds(i * QB, QB), False)
        part(k_ref, v_ref, k_t, dk_ref, dv_ref, cols, True)

    @pl.when(core == 1)
    def _():
        kp_t[...] = transposed(kp_ref[...])
        dkp_acc[...] = jnp.zeros_like(dkp_acc)
        dvp_acc[...] = jnp.zeros_like(dvp_acc)
        for j in range(ROWS // QB):
            block(j, True)
        dkp_ref[...] = dkp_acc[...].astype(BF)
        dvp_ref[...] = dvp_acc[...].astype(BF)

    @pl.when(core == 0)
    def _():
        dkp_ref[...] = jnp.zeros_like(dkp_ref)
        dvp_ref[...] = jnp.zeros_like(dvp_ref)
        for j in range(ROWS // QB):
            block(j, False)

    dq_ref[...] = dq_t[...].T * SCALE


def attention_backward(*args):
    row = sds((ROWS, 128), F32)
    low = sds((ROWS, 128), BF)
    return call(
        attention_backward_kernel,
        "attention_backward",
        None,
        [row, row, row, low, low],
        [
            pltpu.VMEM((128, ROWS), F32),
            pltpu.VMEM((128, ROWS), BF),
            pltpu.VMEM((128, ROWS), BF),
            pltpu.VMEM((2, ROWS), F32),
            pltpu.VMEM((ROWS, 128), F32),
            pltpu.VMEM((ROWS, 128), F32),
        ],
        *args,
    )


def rotary_tables(positions):
    frequency = 10000.0 ** (-(jnp.arange(ROT // 2, dtype=F32) * 2.0) / ROT)
    angles = positions.astype(F32)[:, None] * frequency[None, :]
    cosine, sine = jnp.cos(angles), jnp.sin(angles)
    none = jnp.zeros_like(sine)
    rest = jnp.zeros((positions.shape[0], HD - ROT), F32)
    keep = jnp.concatenate([cosine, cosine, rest + 1.0] * 2, axis=1)
    upper = jnp.concatenate([-sine, none, rest] * 2, axis=1)
    lower = jnp.concatenate([none, sine, rest] * 2, axis=1)
    return keep, upper, lower


def turn(value, tables):
    keep, upper, lower = tables
    return value * keep + jnp.roll(value, -8, axis=1) * upper + jnp.roll(value, 8, axis=1) * lower


def turn_back(value, tables):
    keep, upper, lower = tables
    return value * keep - jnp.roll(value, -8, axis=1) * upper - jnp.roll(value, 8, axis=1) * lower


def normalize(residual):
    mean = jnp.mean(residual, axis=1, keepdims=True)
    centered = residual - mean
    variance = jnp.mean(centered * centered, axis=1, keepdims=True)
    rstd = lax.rsqrt(variance + EPS)
    return centered * rstd, rstd


PAIR_UP = [(2 * i, 2 * i + 1) for i in range(8)]
PAIR_DOWN = [(2 * i + 1, 2 * i) for i in range(8)]


def local(
    tokens, qkv_weight, qkv_bias, out_weight, up_weight, up_bias, down_weight,
    norm_gain, norm_shift, out_bias, cotangent,
):
    core = lax.axis_index("dp") % 2
    tables = rotary_tables(core * ROWS + jnp.arange(ROWS, dtype=jnp.int32))
    gains, shifts = norm_gain.astype(F32), norm_shift.astype(F32)
    weights = []
    for l in range(LAYERS):
        shard = jnp.concatenate(
            [qkv_weight[l].reshape(64, 384), up_weight[l], out_weight[l], down_weight[l]], axis=1
        )
        weights.append(weights_gather(shard, l))
    residual = tokens.astype(F32)
    saved = []
    for l in range(LAYERS):
        w = weights[l]
        normed, rstd = normalize(residual)
        normed_rows = rows_gather(normed.astype(BF), 2 + l)
        wide = normed_rows.astype(F32)
        attn_in = (wide * gains[l, 0] + shifts[l, 0]).astype(BF)
        mlp_in = (wide * gains[l, 1] + shifts[l, 1]).astype(BF)
        projected = dot(attn_in, w[:, 0:384]) + qkv_bias[l].astype(F32).reshape(384)
        q = (turn(projected[:, 0:128], tables) * SCALE).astype(BF)
        k = turn(projected[:, 128:256], tables).astype(BF)
        v = projected[:, 256:384].astype(BF)
        kp, vp = lax.ppermute(jnp.stack([k, v]), "dp", PAIR_UP)
        attended, lse = attention_forward(q, k, v, kp, vp)
        hidden = dot(mlp_in, w[:, 384:896]) + up_bias[l].astype(F32)
        cdf = 0.5 * (1.0 + lax.erf(hidden * (0.5 ** 0.5)))
        activated = (hidden * cdf).astype(BF)
        slope = cdf + hidden * (jnp.exp(-0.5 * hidden * hidden) * (0.5 / jnp.pi) ** 0.5)
        branch = dot(attended, w[:, 896:1024], NT) + dot(activated, w[:, 1024:1536], NT)
        saved.append((normed, rstd, normed_rows, attn_in, mlp_in, q, k, v, kp, vp, lse, attended, activated, slope))
        residual = residual + rows_scatter(branch.astype(BF), 4 + l) + out_bias[l].astype(F32)
    output = residual.astype(BF)
    grad = cotangent.astype(F32)
    weight_grads = [None] * LAYERS
    along = [None] * LAYERS
    every = [None] * LAYERS
    for l in reversed(range(LAYERS)):
        w = weights[l]
        normed, rstd, normed_rows, attn_in, mlp_in, q, k, v, kp, vp, lse, attended, activated, slope = saved[l]
        out_bias_part = jnp.sum(grad, axis=0)
        grad_rows = rows_gather(grad.astype(BF), 6 + l)
        out_part = dot(grad_rows, attended, TN).astype(BF)
        down_part = dot(grad_rows, activated, TN).astype(BF)
        attended_grad = dot(grad_rows, w[:, 896:1024]).astype(BF)
        activated_grad = dot(grad_rows, w[:, 1024:1536]).astype(BF)
        hidden_grad = (activated_grad.astype(F32) * slope).astype(BF)
        dq, dk, dv, dkp, dvp = attention_backward(q, k, v, kp, vp, lse, attended, attended_grad)
        back_k, back_v = lax.ppermute(jnp.stack([dkp, dvp]), "dp", PAIR_DOWN)
        projected_grad = jnp.concatenate(
            [
                turn_back(dq, tables),
                turn_back(dk + back_k.astype(F32), tables),
                dv + back_v.astype(F32),
            ],
            axis=1,
        ).astype(BF)
        qkv_part = dot(attn_in, projected_grad, TN).astype(BF)
        up_part = dot(mlp_in, hidden_grad, TN).astype(BF)
        attn_back = dot(projected_grad, w[:, 0:384], NT)
        mlp_back = dot(hidden_grad, w[:, 384:896], NT)
        wide = normed_rows.astype(F32)
        every[l] = jnp.stack(
            [
                jnp.sum(attn_back * wide, axis=0),
                jnp.sum(mlp_back * wide, axis=0),
                jnp.sum(attn_back, axis=0),
                jnp.sum(mlp_back, axis=0),
                out_bias_part,
            ]
        )
        along[l] = jnp.concatenate(
            [jnp.sum(projected_grad.astype(F32), axis=0), jnp.sum(hidden_grad.astype(F32), axis=0)]
        )
        normed_grad = rows_scatter((attn_back * gains[l, 0] + mlp_back * gains[l, 1]).astype(BF), 8 + l)
        grad = grad + rstd * (
            normed_grad
            - jnp.mean(normed_grad, axis=1, keepdims=True)
            - normed * jnp.mean(normed_grad * normed, axis=1, keepdims=True)
        )
        weight_grads[l] = weights_scatter(
            jnp.concatenate([qkv_part, up_part, out_part, down_part], axis=1), 10 + l
        )
    every_sum, along_sum = small_sums(
        jnp.stack(every).reshape(8, 10, 128), jnp.stack(along).reshape(14, 128), 12
    )
    every_sum = every_sum.reshape(LAYERS, 5, D)
    along_sum = along_sum.reshape(LAYERS, 896)
    grads = jnp.stack(weight_grads)
    return (
        output,
        grad,
        grads[:, :, 0:384].reshape(LAYERS, 64, 3, 128),
        along_sum[:, 0:384].reshape(LAYERS, 3, 128),
        grads[:, :, 896:1024],
        grads[:, :, 384:896],
        along_sum[:, 384:896],
        grads[:, :, 1024:1536],
        every_sum[:, 0:2],
        every_sum[:, 2:4],
        every_sum[:, 4],
    )


def solution(mesh):
    in_specs = (
        P(("dp", "tensor"), None),
        P(None, "dp", None, "tensor"),
        P(None, None, "tensor"),
        P(None, "dp", "tensor"),
        P(None, "dp", "tensor"),
        P(None, "tensor"),
        P(None, "dp", "tensor"),
        P(),
        P(),
        P(),
        P(("dp", "tensor"), None),
    )
    out_specs = (
        P(("dp", "tensor"), None),
        P(("dp", "tensor"), None),
        P(None, "dp", None, "tensor"),
        P(None, None, "tensor"),
        P(None, "dp", "tensor"),
        P(None, "dp", "tensor"),
        P(None, "tensor"),
        P(None, "dp", "tensor"),
        P(),
        P(),
        P(),
    )
    return jax.shard_map(local, mesh=mesh, in_specs=in_specs, out_specs=out_specs, check_vma=False)
```

time: 1420 us -> 596 us (0.42)
  waiting for transfers between devices: 866 us -> 0.01 us
  Pallas kernels: 0 us -> 416 us
  blocking collectives: 222 us -> 0 us
  matrix products: 158 us -> 70.2 us
  other arithmetic: 67.3 us -> 44.7 us
  starting transfers between devices: 31.5 us -> 13.4 us
  local copies, waits for them, and re-layouts: 57.2 us -> 40.1 us
  between operations: 16.3 us -> 1.97 us
    reduce_scatter x14 -> x0, waiting for transfers between devices: 589 us -> none  [the longest x2 138 us: local(): lax.psum_scatter(up_grad.astype(jnp.bfloat16), 'dp', scatter_dimension=0,...]
    pallas_call x0 -> x17, Pallas kernels: none -> 416 us  [call(): pl.pallas_call(kernel, name=name, out_shape=out, in_specs=[VM] * len(args...]
    all_gather x10 -> x0, waiting for transfers between devices: 260 us -> none  [the longest x2 73.3 us: local(): lax.all_gather(mlp_in.astype(jnp.bfloat16), 'tensor', axis=0, tiled=True)]
    all_gather x4 -> x0, blocking collectives: 117 us -> none  [the longest x2 75.9 us: local(): lax.all_gather(qkv_weight[layer_index], 'dp', axis=0, tiled=True)]
    psum x2 -> x0, blocking collectives: 105 us -> none  [the longest x1 69.3 us: local(): lax.psum((jnp.stack(gain_terms), jnp.stack(shift_terms), jnp.stack(out_bi...]
    dot_general x52 -> x24, matrix products: 158 us -> 70.2 us  [dot(): return lax.dot_general(a, b, dims, preferred_element_type=F32)]
    dynamic_update_slice x8 -> x0, local copies, waits for them, and re-layouts: 24.1 us -> none  [attention_forward(): lax.map(one_block, (queries.reshape(block_count, block_rows, head_count,...]
    reduce_sum x16 -> x9, other arithmetic: 25.7 us -> 8.65 us  [the longest x2 2.53 us: local(): jnp.mean(normed_grad, axis=1, keepdims=True)]
  transfers between devices with their start and end apart: 28 -> 4, of which waited for: 22 -> 0; matrix products, arithmetic and copies ran while one was open for 17% -> 7% of each run, Pallas kernels for 0% -> 14%
where the time goes in v1:
time: 596 us; the launch traced here: 586 us
  Pallas kernels  416 us (70%)
  matrix products  70.2 us (12%)
  other arithmetic  44.7 us (8%)
  local copies, waits for them, and re-layouts  40.1 us (7%)
  starting transfers between devices  13.4 us (2%)
    pallas_call x17, Pallas kernels, call(): pl.pallas_call(kernel, name=name, out_shape=out, in_specs=[VM] * len(args...  416 us
    dot_general x24, matrix products, dot(): return lax.dot_general(a, b, dims, preferred_element_type=F32)  70.2 us
  transfers between devices with their start and end apart: 4, of which 0 were waited for; matrix products, arithmetic and copies ran while one was open for 7% of the time, Pallas kernels for 14%

profile of v1, /device:TPU:1, one launch (start us, length us, event | category | flops | bytes accessed | tf_op | source)
XLA Modules:
  0.0 586.4 jit_solution(10973526663133941230)
XLA Ops:
  5.0 24.0 %rows_gather.4 = bf16[8,128,1024]{2,1,0:T(8,128)(2,1)} custom-call(bf16[128,1024]{1,0:T(8,128)(2,1)} %fusion.51.x_ref), custom_call_target="tpu_custom_call" | custom-call | tf_op jit(solution)/shard_map/rows_gather/pallas_call | solution.py:52
  30.0 29.7 %weights_gather.2 = bf16[16,64,1536]{2,1,0:T(8,128)(2,1)} custom-call(bf16[64,1536]{1,0:T(8,128)(2,1)} %get-tuple-element.189.x_ref), custom_call_target="tpu_custom_call" | custom-call | tf_op jit(solution)/shard_map/weights_gather/pallas_call | solution.py:52
  59.7 2.6 fusion.1
  62.3 3.0 convolution_add_fusion.1
  69.3 3.1 multiply_sine_fusion
  72.5 2.1 concatenate.88
  74.7 2.2 concatenate.90
  77.7 2.7 concatenate.86
  80.4 3.5 fusion.67
  86.8 25.5 %weights_gather.3 = bf16[16,64,1536]{2,1,0:T(8,128)(2,1)} custom-call(bf16[64,1536]{1,0:T(8,128)(2,1)} %get-tuple-element.190.x_ref), custom_call_target="tpu_custom_call" | custom-call | tf_op jit(solution)/shard_map/weights_gather/pallas_call | solution.py:52
  112.4 23.8 %rows_gather.6 = bf16[8,128,1024]{2,1,0:T(8,128)(2,1)} custom-call(bf16[128,1024]{1,0:T(8,128)(2,1)} %x_ref), custom_call_target="tpu_custom_call" | custom-call | tf_op jit(solution)/shard_map/rows_gather/pallas_call | solution.py:52
  136.2 4.5 multiply_convert_fusion.1
  140.7 2.6 fusion.26.do_ref
  143.3 3.3 fusion.35
  147.3 10.9 %attention_forward.2 = (bf16[1024,128]{1,0:T(8,128)(2,1)}, f32[2,1024]{1,0:T(2,128)}) custom-call(bf16[1024,128]{1,0:T(8,128)(2,1)} %get-tuple-element.103.q_ref, bf16[1024,128]{1,0:T(8,128)(2,1)} %copy-done.9, bf16[1024,128]{1,0:T(8,128)(2,1)} %slice.499.v_ref, bf16[1024,128]{1,0:T(8,128)(2,1)} %get-tuple-element.154.kp_ref, ...), custom_call_target="tpu_custom_call" | custom-call | tf_op jit(solution)/shard_map/attention_forward/pallas_call | solution.py:52
  158.3 4.4 add_convert_fusion.3
  162.7 31.3 %rows_scatter.4 = f32[128,1024]{1,0:T(8,128)} custom-call(bf16[8,128,1024]{2,1,0:T(8,128)(2,1)} %bitcast.162), custom_call_target="tpu_custom_call" | custom-call | tf_op jit(solution)/shard_map/rows_scatter/pallas_call | solution.py:52
  196.2 23.4 %rows_gather.5 = bf16[8,128,1024]{2,1,0:T(8,128)(2,1)} custom-call(bf16[128,1024]{1,0:T(8,128)(2,1)} %fusion.86.x_ref), custom_call_target="tpu_custom_call" | custom-call | tf_op jit(solution)/shard_map/rows_gather/pallas_call | solution.py:52
  219.7 2.8 fusion.7
  224.6 2.3 multiply_convert_fusion
  228.2 3.3 fusion.28
  236.2 2.3 convolution_convert_fusion.2
  239.2 3.3 fusion.30
  243.3 8.8 %attention_forward.3 = (bf16[1024,128]{1,0:T(8,128)(2,1)}, f32[2,1024]{1,0:T(2,128)}) custom-call(bf16[1024,128]{1,0:T(8,128)(2,1)} %get-tuple-element.101.q_ref, bf16[1024,128]{1,0:T(8,128)(2,1)} %copy-done.10, bf16[1024,128]{1,0:T(8,128)(2,1)} %slice.498.v_ref, bf16[1024,128]{1,0:T(8,128)(2,1)} %get-tuple-element.152.kp_ref, ...), custom_call_target="tpu_custom_call" | custom-call | tf_op jit(solution)/shard_map/attention_forward/pallas_call | solution.py:52
  252.1 16.7 %attention_backward.2 = (f32[1024,128]{1,0:T(8,128)}, f32[1024,128]{1,0:T(8,128)}, f32[1024,128]{1,0:T(8,128)}, bf16[1024,128]{1,0:T(8,128)(2,1)}, bf16[1024,128]{1,0:T(8,128)(2,1)}) custom-call(bf16[1024,128]{1,0:T(8,128)(2,1)} %get-tuple-element.101.q_ref, bf16[1024,128]{1,0:T(8,128)(2,1)} %copy-done.10, bf16[1024,128]{1,0:T(8,128)(2,1)} %slice.498.v_ref, ...), custom_call_target="tpu_custom_call" | custom-call | tf_op jit(solution)/shard_map/attention_backward/pallas_call | solution.py:52
  269.9 8.6 %collective-permute-start.2 = (bf16[2,1024,128]{2,1,0:T(8,128)(2,1)S(1)}, bf16[2,1024,128]{2,1,0:T(8,128)(2,1)}, u32[]{:S(2)}, u32[]{:S(2)}) collective-permute-start(bf16[2,1024,128]{2,1,0:T(8,128)(2,1)S(1)} %pad_maximum_fusion.6), channel_id=1, source_target_pairs={{8,0},{24,16},{40,32},{56,48},{72,64},{88,80},{104,96},{120,112},{... | collective-permute-start | bytes 1572872 | tf_op jit(solution)/shard_map/ppermute | solution.py:549
  279.9 4.4 add_convert_fusion.2
  284.3 35.2 %rows_scatter.5 = f32[128,1024]{1,0:T(8,128)} custom-call(bf16[8,128,1024]{2,1,0:T(8,128)(2,1)} %bitcast.163), custom_call_target="tpu_custom_call" | custom-call | tf_op jit(solution)/shard_map/rows_scatter/pallas_call | solution.py:52
  327.0 4.4 fusion.98
  331.4 38.4 %rows_scatter.6 = f32[128,1024]{1,0:T(8,128)} custom-call(bf16[8,128,1024]{2,1,0:T(8,128)(2,1)} %bitcast.189), custom_call_target="tpu_custom_call" | custom-call | tf_op jit(solution)/shard_map/rows_scatter/pallas_call | solution.py:52
  373.8 22.8 %rows_gather.7 = bf16[8,128,1024]{2,1,0:T(8,128)(2,1)} custom-call(bf16[128,1024]{1,0:T(8,128)(2,1)} %convert_element_type.255.x_ref), custom_call_target="tpu_custom_call" | custom-call | tf_op jit(solution)/shard_map/rows_gather/pallas_call | solution.py:52
  396.6 3.2 convolution_convert_fusion.11.do_ref
  401.0 2.3 convolution_convert_fusion.3
  405.4 4.6 copy.49
  410.1 28.3 %weights_scatter.3 = f32[64,1536]{1,0:T(8,128)} custom-call(bf16[16,64,1536]{2,1,0:T(8,128)(2,1)} %bitcast.160), custom_call_target="tpu_custom_call" | custom-call | tf_op jit(solution)/shard_map/weights_scatter/pallas_call | solution.py:52
  438.4 16.3 %attention_backward.3 = (f32[1024,128]{1,0:T(8,128)}, f32[1024,128]{1,0:T(8,128)}, f32[1024,128]{1,0:T(8,128)}, bf16[1024,128]{1,0:T(8,128)(2,1)}, bf16[1024,128]{1,0:T(8,128)(2,1)}) custom-call(bf16[1024,128]{1,0:T(8,128)(2,1)} %get-tuple-element.103.q_ref, bf16[1024,128]{1,0:T(8,128)(2,1)} %copy-done.9, bf16[1024,128]{1,0:T(8,128)(2,1)} %slice.499.v_ref, ...), custom_call_target="tpu_custom_call" | custom-call | tf_op jit(solution)/shard_map/attention_backward/pallas_call | solution.py:52
  456.6 2.3 collective-permute-start.3
  458.8 2.2 fusion.109
  461.0 3.4 convert_reduce_fusion.1
  464.5 2.3 convolution_convert_fusion.4
  468.1 4.6 fusion.37
  479.4 6.7 %fusion.96 = (f32[1024]{0:T(1024)S(1)}, f32[1024]{0:T(1024)S(1)}, bf16[1024,1024]{1,0:T(8,128)(2,1)}, f32[1024]{0:T(1024)S(1)}, f32[1024]{0:T(1024)S(1)}) fusion(f32[1024,1024]{1,0:T(8,128)} %fusion.37, bf16[8,128,1024]{2,1,0:T(8,128)(2,1)} %rows_gather.4, f32[1024]{0:T(1024)S(1)} %bitcast.209, f32[1024]{0:T(1024)S(1)} %bitcast.207, ...), kind=kOutput, calls=%fused_computation.225 | convolution fusion | flops 819195904 | bytes 9986048 | tf_op jit(solution)/shard_map/dot_general | solution.py:29
  486.8 17.5 %small_sums.1 = (f32[8,10,128]{2,1,0:T(8,128)}, f32[14,128]{1,0:T(8,128)}) custom-call(f32[8,10,128]{2,1,0:T(8,128)} %reshape.169.every_ref, f32[14,128]{1,0:T(8,128)} %reshape.170.along_ref), custom_call_target="tpu_custom_call" | custom-call | tf_op jit(solution)/shard_map/small_sums/pallas_call | solution.py:52
  505.8 3.0 pad_maximum_fusion
  508.9 4.6 copy.48
  513.5 28.1 %weights_scatter.2 = f32[64,1536]{1,0:T(8,128)} custom-call(bf16[16,64,1536]{2,1,0:T(8,128)(2,1)} %bitcast.161), custom_call_target="tpu_custom_call" | custom-call | tf_op jit(solution)/shard_map/weights_scatter/pallas_call | solution.py:52
  547.4 35.2 %rows_scatter.7 = f32[128,1024]{1,0:T(8,128)} custom-call(bf16[8,128,1024]{2,1,0:T(8,128)(2,1)} %bitcast.188), custom_call_target="tpu_custom_call" | custom-call | tf_op jit(solution)/shard_map/rows_scatter/pallas_call | solution.py:52
  583.9 2.1 fusion.55
  (209 shorter events, 61.9 us)
Async XLA Ops:
  0.6 28.3 %copy-start.43 = (bf16[2,2,1024]{2,1,0:T(2,128)(2,1)S(1)}, bf16[2,2,1024]{2,1,0:T(2,128)(2,1)}, u32[]{:S(2)}) copy-start(bf16[2,2,1024]{2,1,0:T(2,128)(2,1)} %param.18) | copy-start | bytes 24580
  0.7 28.3 %copy-start.44 = (bf16[2,2,1024]{2,1,0:T(2,128)(2,1)S(1)}, bf16[2,2,1024]{2,1,0:T(2,128)(2,1)}, u32[]{:S(2)}) copy-start(bf16[2,2,1024]{2,1,0:T(2,128)(2,1)} %param.19) | copy-start | bytes 24580
  0.7 28.3 %copy-start.41 = (bf16[2,64,3,128]{3,1,2,0:T(8,128)(2,1)S(1)}, bf16[2,64,3,128]{3,1,2,0:T(8,128)(2,1)}, u32[]{:S(2)}) copy-start(bf16[2,64,3,128]{3,1,2,0:T(8,128)(2,1)} %param.12) | copy-start | bytes 294916
  0.7 28.5 %copy-start.39 = (bf16[2,64,512]{2,1,0:T(8,128)(2,1)S(1)}, bf16[2,64,512]{2,1,0:T(8,128)(2,1)}, u32[]{:S(2)}) copy-start(bf16[2,64,512]{2,1,0:T(8,128)(2,1)} %param.15) | copy-start | bytes 393220
  1.8 27.3 %copy-start.40 = (bf16[2,64,512]{2,1,0:T(8,128)(2,1)S(1)}, bf16[2,64,512]{2,1,0:T(8,128)(2,1)}, u32[]{:S(2)}) copy-start(bf16[2,64,512]{2,1,0:T(8,128)(2,1)} %param.17) | copy-start | bytes 393220
  3.1 26.1 %copy-start.42 = (bf16[2,64,128]{2,1,0:T(8,128)(2,1)S(1)}, bf16[2,64,128]{2,1,0:T(8,128)(2,1)}, u32[]{:S(2)}) copy-start(bf16[2,64,128]{2,1,0:T(8,128)(2,1)} %param.14) | copy-start | bytes 98308
  29.2 30.5 %copy-start.48 = (bf16[2,3,128]{2,0,1:T(2,128)(2,1)S(1)}, bf16[2,3,128]{2,0,1:T(2,128)(2,1)}, u32[]{:S(2)}) copy-start(bf16[2,3,128]{2,0,1:T(2,128)(2,1)} %param.13) | copy-start | bytes 4612
  29.3 30.5 %copy-start.5 = (bf16[8,128,1024]{2,1,0:T(8,128)(2,1)S(1)}, bf16[8,128,1024]{2,1,0:T(8,128)(2,1)}, u32[]{:S(2)}) copy-start(bf16[8,128,1024]{2,1,0:T(8,128)(2,1)} %rows_gather.4) | copy-start | bytes 6291460
  62.3 3.0 copy-start.15
  80.4 3.5 copy-start.29
  80.4 6.4 %copy-start.46 = (bf16[2,512]{1,0:T(2,128)(2,1)S(1)}, bf16[2,512]{1,0:T(2,128)(2,1)}, u32[]{:S(2)}) copy-start(bf16[2,512]{1,0:T(2,128)(2,1)} %param.16) | copy-start | bytes 6148
  83.9 28.4 %copy-start.9 = (bf16[1024,128]{1,0:T(8,128)(2,1)}, bf16[1024,128]{1,0:T(8,128)(2,1)S(1)}, u32[]{:S(2)}) copy-start(bf16[1024,128]{1,0:T(8,128)(2,1)S(1)} %get-tuple-element.102.k_ref) | copy-start | bytes 786436
  84.8 61.7 %collective-permute-start = (bf16[2,1024,128]{2,1,0:T(8,128)(2,1)}, bf16[2,1024,128]{2,1,0:T(8,128)(2,1)S(1)}, u32[]{:S(2)}, u32[]{:S(2)}) collective-permute-start(bf16[2,1024,128]{2,1,0:T(8,128)(2,1)} %pad_maximum_fusion.4), channel_id=1, source_target_pairs={{0,8},{16,24},{32,40},{48,56},{64,72},{80,88},{96,104},{112,120},{... | collective-permute-start | bytes 1572872 | tf_op jit(solution)/shard_map/ppermute | solution.py:524
  86.8 49.3 %copy-start.11 = (bf16[16,64,1536]{2,1,0:T(8,128)(2,1)S(1)}, bf16[16,64,1536]{2,1,0:T(8,128)(2,1)}, u32[]{:S(2)}) copy-start(bf16[16,64,1536]{2,1,0:T(8,128)(2,1)} %weights_gather.2) | copy-start | bytes 9437188
  136.2 4.5 copy-start
  140.7 5.9 %copy-start.50 = (bf16[1024,512]{1,0:T(8,128)(2,1)}, bf16[1024,512]{1,0:T(8,128)(2,1)S(1)}, u32[]{:S(2)}) copy-start(bf16[1024,512]{1,0:T(8,128)(2,1)S(1)} %get-tuple-element.181) | copy-start | bytes 3145732
  140.7 2.6 copy-start.45
  162.7 31.3 %copy-start.4 = (bf16[128,1024]{1,0:T(8,128)(2,1)S(1)}, bf16[128,1024]{1,0:T(8,128)(2,1)}, u32[]{:S(2)}) copy-start(bf16[128,1024]{1,0:T(8,128)(2,1)} %param.11) | copy-start | bytes 786436
  219.7 2.9 copy-start.12
  232.9 3.3 copy-start.10
  233.0 9.5 %collective-permute-start.1 = (bf16[2,1024,128]{2,1,0:T(8,128)(2,1)S(1)}, bf16[2,1024,128]{2,1,0:T(8,128)(2,1)S(1)}, u32[]{:S(2)}, u32[]{:S(2)}) collective-permute-start(bf16[2,1024,128]{2,1,0:T(8,128)(2,1)S(1)} %pad_maximum_fusion.5), channel_id=1, source_target_pairs={{0,8},{16,24},{32,40},{48,56},{64,72},{80,88},{96,104},{112,120},{... | collective-permute-start | bytes 1572872 | tf_op jit(solution)/shard_map/ppermute | solution.py:524
  252.1 27.8 %copy-start.13 = (bf16[1024,128]{1,0:T(8,128)(2,1)S(1)}, bf16[1024,128]{1,0:T(8,128)(2,1)}, u32[]{:S(2)}) copy-start(bf16[1024,128]{1,0:T(8,128)(2,1)} %get-tuple-element.28.o_ref) | copy-start | bytes 786436
  269.9 50.3 %collective-permute-start.2 = (bf16[2,1024,128]{2,1,0:T(8,128)(2,1)S(1)}, bf16[2,1024,128]{2,1,0:T(8,128)(2,1)}, u32[]{:S(2)}, u32[]{:S(2)}) collective-permute-start(bf16[2,1024,128]{2,1,0:T(8,128)(2,1)S(1)} %pad_maximum_fusion.6), channel_id=1, source_target_pairs={{8,0},{24,16},{40,32},{56,48},{72,64},{88,80},{104,96},{120,112},{... | collective-permute-start | bytes 1572872 | tf_op jit(solution)/shard_map/ppermute | solution.py:549
  284.3 35.3 %copy-start.2 = (f32[1024,128]{1,0:T(8,128)S(1)}, f32[1024,128]{1,0:T(8,128)}, u32[]{:S(2)}) copy-start(f32[1024,128]{1,0:T(8,128)} %get-tuple-element.30) | copy-start | bytes 1572868
  322.9 2.9 copy-start.24
  323.9 3.1 copy-start.49
  331.4 39.7 %copy-start.22 = (f32[128,1024]{1,0:T(8,128)S(1)}, f32[128,1024]{1,0:T(8,128)}, u32[]{:S(2)}) copy-start(f32[128,1024]{1,0:T(8,128)} %rows_scatter.5) | copy-start | bytes 1572868
  331.4 39.7 %copy-start.23 = (bf16[128,1024]{1,0:T(8,128)(2,1)S(1)}, bf16[128,1024]{1,0:T(8,128)(2,1)}, u32[]{:S(2)}) copy-start(bf16[128,1024]{1,0:T(8,128)(2,1)} %x_ref) | copy-start | bytes 786436
  373.8 25.9 %copy-start.32 = (bf16[1024,128]{1,0:T(8,128)(2,1)S(1)}, bf16[1024,128]{1,0:T(8,128)(2,1)}, u32[]{:S(2)}) copy-start(bf16[1024,128]{1,0:T(8,128)(2,1)} %get-tuple-element.27.o_ref) | copy-start | bytes 786436
  396.5 3.2 copy-start.20
  400.9 2.5 copy-start.31
  400.9 2.5 copy-start.33
  438.4 22.6 %copy-start.21 = (bf16[8,128,1024]{2,1,0:T(8,128)(2,1)S(1)}, bf16[8,128,1024]{2,1,0:T(8,128)(2,1)}, u32[]{:S(2)}) copy-start(bf16[8,128,1024]{2,1,0:T(8,128)(2,1)} %rows_gather.7) | copy-start | bytes 6291460
  438.4 22.6 %copy-start.54 = (f32[1024,512]{1,0:T(8,128)S(1)}, f32[1024,512]{1,0:T(8,128)}, u32[]{:S(2)}) copy-start(f32[1024,512]{1,0:T(8,128)} %get-tuple-element.182) | copy-start | bytes 6291460
  456.6 16.1 %collective-permute-start.3 = (bf16[2,1024,128]{2,1,0:T(8,128)(2,1)}, bf16[2,1024,128]{2,1,0:T(8,128)(2,1)}, u32[]{:S(2)}, u32[]{:S(2)}) collective-permute-start(bf16[2,1024,128]{2,1,0:T(8,128)(2,1)} %pad_maximum_fusion.7), channel_id=1, source_target_pairs={{8,0},{24,16},{40,32},{56,48},{72,64},{88,80},{104,96},{120,112},{... | collective-permute-start | bytes 1572872 | tf_op jit(solution)/shard_map/ppermute | solution.py:549
  461.0 3.4 copy-start.17
  464.4 2.4 copy-start.52
  464.5 2.4 copy-start.1
  468.1 4.6 copy-start.34
  468.1 4.6 copy-start.35
  473.9 4.7 copy-start.26
  475.7 2.8 copy-start.27
  475.7 2.8 copy-start.28
  479.4 26.4 %copy-start.30 = (bf16[1024,512]{0,1:T(8,128)(2,1)S(1)}, bf16[1024,512]{0,1:T(8,128)(2,1)}, u32[]{:S(2)}) copy-start(bf16[1024,512]{0,1:T(8,128)(2,1)} %convolution_convert_fusion.3) | copy-start | bytes 3145732
  479.4 26.4 %copy-start.38 = (bf16[1024,128]{0,1:T(8,128)(2,1)S(1)}, bf16[1024,128]{0,1:T(8,128)(2,1)}, u32[]{:S(2)}) copy-start(bf16[1024,128]{0,1:T(8,128)(2,1)} %convolution_convert_fusion.10) | copy-start | bytes 786436
  513.5 28.1 %copy-start.7 = (f32[64,1536]{1,0:T(8,128)S(1)}, f32[64,1536]{1,0:T(8,128)}, u32[]{:S(2)}) copy-start(f32[64,1536]{1,0:T(8,128)} %weights_scatter.3) | copy-start | bytes 1179652
  513.5 31.4 %copy-start.47 = (f32[14,128]{1,0:T(8,128)S(1)}, f32[14,128]{1,0:T(8,128)}, u32[]{:S(2)}) copy-start(f32[14,128]{1,0:T(8,128)} %get-tuple-element.41) | copy-start | bytes 21508
  541.6 4.5 copy-start.8
  (11 other events, 16.8 us)

commit v2 on v1

v2 whole, which is shorter than its diff:
```python
import functools

import jax
import jax.numpy as jnp
from jax import lax
from jax.experimental import pallas as pl
from jax.experimental.pallas import tpu as pltpu
from jax.sharding import PartitionSpec as P

BF = jnp.bfloat16
F32 = jnp.float32
D = 1024
HD = 64
ROT = 16
LAYERS = 2
ROWS = 1024
QB = 256
EPS = 1e-05
MASKED = -1e30
SCALE = HD ** (-0.5)
VM = pl.BlockSpec(memory_space=pltpu.VMEM)
DMA = pltpu.SemaphoreType.DMA
NN = (((1,), (0,)), ((), ()))
NT = (((1,), (1,)), ((), ()))
TN = (((0,), (0,)), ((), ()))


def dot(a, b, dims=NN):
    return lax.dot_general(a, b, dims, preferred_element_type=F32)


def remote(src, dst, send, recv, dp, tensor):
    return pltpu.make_async_remote_copy(
        src_ref=src,
        dst_ref=dst,
        send_sem=send,
        recv_sem=recv,
        device_id=(dp, tensor),
        device_id_type=pl.DeviceIdType.MESH,
    )


def greet(peers):
    sem = pltpu.get_barrier_semaphore()
    for peer in peers:
        pl.semaphore_signal(sem, inc=1, device_id=peer, device_id_type=pl.DeviceIdType.MESH)
    pl.semaphore_wait(sem, len(peers))


def call(kernel, name, cid, out, scratch, *args):
    many = isinstance(out, (list, tuple))
    return pl.pallas_call(
        kernel,
        name=name,
        out_shape=out,
        in_specs=[VM] * len(args),
        out_specs=[VM] * len(out) if many else VM,
        scratch_shapes=scratch,
        compiler_params=pltpu.CompilerParams(
            collective_id=cid, has_side_effects=cid is not None, vmem_limit_bytes=56 << 20
        ),
    )(*args)


def sds(shape, dtype):
    return jax.ShapeDtypeStruct(shape, dtype)


def place():
    return lax.axis_index("dp"), lax.axis_index("tensor")


def sibling_of(dp):
    return dp + 1 - 2 * (dp % 2)


GROUP = [(2, 1), (1, 1), (3, 1), (2, 0), (0, 1), (1, 0), (3, 0)]
STEPS = (1, 3, 2)
CHIPS = [(2, 1), (1, 1), (3, 1), (0, 1), (2, 0), (1, 0), (3, 0)]


def group_peers(dp, t):
    x, y = t % 4, t // 4
    return [(dp, ((y + dy) % 2) * 4 + (x + dx) % 4) for dx, dy in GROUP]


def weight_peers(dp, t):
    z, yh, core = dp // 4, (dp // 2) % 2, dp % 2
    return [(z * 4 + (1 - yh) * 2 + core, t)] + [(((z + d) % 4) * 4 + yh * 2 + core, t) for d in STEPS]


def chip_peers(dp, t):
    z, yh, core = dp // 4, (dp // 2) % 2, dp % 2
    return [(((z + dz) % 4) * 4 + ((yh + dy) % 2) * 2 + core, t) for dz, dy in CHIPS]


class RowsGather:
    def __init__(self, o_ref, ss, rs):
        self.o, self.ss, self.rs = o_ref, ss, rs
        self.dp, self.t = place()
        x, y = self.t % 4, self.t // 4
        self.right, self.left, self.across = y * 4 + (x + 1) % 4, y * 4 + (x + 3) % 4, (1 - y) * 4 + x
        self.a_right, self.a_left = (1 - y) * 4 + (x + 1) % 4, (1 - y) * 4 + (x + 3) % 4
        self.far, self.a_far = y * 4 + (x + 2) % 4, (1 - y) * 4 + (x + 2) % 4
        self.copies = []

    def send(self, ref, to):
        i = len(self.copies)
        c = remote(ref, ref, self.ss.at[i], self.rs.at[i], self.dp, to)
        c.start()
        self.copies.append(c)
        return c

    def top(self, slot):
        return self.o.at[slot, 0:64]

    def bottom(self, slot):
        return self.o.at[slot, 64:128]

    def start(self):
        own = self.o.at[self.t]
        self.c_across = self.send(own, self.across)
        self.c_right = self.send(own, self.right)
        self.c_left = self.send(own, self.left)
        return [self.t]

    def second(self):
        self.c_across.wait_recv()
        block = self.o.at[self.across]
        self.d_right = self.send(block, self.right)
        self.d_left = self.send(block, self.left)
        return [self.across]

    def third(self):
        self.c_right.wait_recv()
        self.e_right = self.send(self.top(self.left), self.right)
        self.c_left.wait_recv()
        self.e_left = self.send(self.bottom(self.right), self.left)
        return [self.left, self.right]

    def fourth(self):
        self.d_right.wait_recv()
        self.f_right = self.send(self.top(self.a_left), self.right)
        self.d_left.wait_recv()
        self.f_left = self.send(self.bottom(self.a_right), self.left)
        return [self.a_left, self.a_right]

    def fifth(self):
        self.e_right.wait_recv()
        self.e_left.wait_recv()
        return [self.far]

    def sixth(self):
        self.f_right.wait_recv()
        self.f_left.wait_recv()
        return [self.a_far]

    def finish(self):
        for c in self.copies:
            c.wait_send()


class RowsScatter:
    def __init__(self, out, got, ss, rs):
        self.out, self.got, self.ss, self.rs = out, got, ss, rs
        self.peers = group_peers(*place())
        self.copies = []

    def send(self, i, value):
        dp, to = self.peers[i]
        self.out[i] = value.astype(BF)
        c = remote(self.out.at[i], self.got.at[i], self.ss.at[i], self.rs.at[i], dp, to)
        c.start()
        self.copies.append(c)

    def finish(self, total):
        for i, c in enumerate(self.copies):
            c.wait_recv()
            total = total + self.got[i].astype(F32)
        for c in self.copies:
            c.wait_send()
        return total


class WeightsGather:
    def __init__(self, x_ref, o_ref, ss, rs):
        self.x, self.o, self.ss, self.rs = x_ref, o_ref, ss, rs
        self.dp, self.t = place()
        self.copies, self.last = [], []

    def rows(self, slot):
        return self.o.at[pl.ds(pl.multiple_of(slot * 64, 64), 64), :]

    def send(self, slot, to, src=None):
        i = len(self.copies)
        block = self.rows(slot)
        c = remote(block if src is None else src, block, self.ss.at[i], self.rs.at[i], to, self.t)
        c.start()
        self.copies.append(c)
        return c

    def start(self):
        dp = self.dp
        peers = [p for p, _ in weight_peers(dp, self.t)]
        self.across, self.ring = peers[0], peers[1:]
        self.c_across = self.send(dp, self.across, self.x)
        self.c_ring = [self.send(dp, q, self.x) for q in self.ring]
        self.last.append(self.send(dp, sibling_of(dp), self.x))
        self.o[pl.ds(pl.multiple_of(dp * 64, 64), 64), :] = self.x[...]

    def second(self):
        self.c_across.wait_recv()
        self.d_ring = [self.send(self.across, q) for q in self.ring]
        self.last.append(self.send(self.across, sibling_of(self.dp)))

    def pass_on(self, group, y_part):
        dp = self.dp
        z, core = dp // 4, dp % 2
        for c, d in zip(group, STEPS):
            c.wait_recv()
            self.last.append(self.send(((z + 4 - d) % 4) * 4 + y_part * 2 + core, sibling_of(dp)))

    def third(self):
        self.pass_on(self.c_ring, (self.dp // 2) % 2)

    def fourth(self):
        self.pass_on(self.d_ring, 1 - (self.dp // 2) % 2)

    def finish(self):
        for c in self.last:
            c.wait_recv()

    def drain(self):
        for c in self.copies:
            c.wait_send()


class WeightsScatter:
    def __init__(self, x_ref, pair, mid, got, ss, rs):
        self.x, self.pair, self.mid, self.got, self.ss, self.rs = x_ref, pair, mid, got, ss, rs
        self.dp, self.t = place()
        self.places = [p for p, _ in chip_peers(self.dp, self.t)] + [self.dp]
        self.inner, self.outer = [], []

    def rows(self, slot):
        return pl.ds(pl.multiple_of(slot * 64, 64), 64)

    def start(self):
        for i, p in enumerate(self.places):
            c = remote(
                self.x.at[self.rows(sibling_of(p)), :], self.pair.at[i], self.ss.at[i], self.rs.at[i],
                sibling_of(self.dp), self.t,
            )
            c.start()
            self.inner.append(c)

    def both(self, i):
        self.inner[i].wait_recv()
        return self.x[self.rows(self.places[i]), :].astype(F32) + self.pair[i].astype(F32)

    def second(self):
        for i in range(7):
            self.mid[i] = self.both(i).astype(BF)
            c = remote(self.mid.at[i], self.got.at[i], self.ss.at[8 + i], self.rs.at[8 + i], self.places[i], self.t)
            c.start()
            self.outer.append(c)

    def finish(self, out):
        total = self.both(7)
        for i, c in enumerate(self.outer):
            c.wait_recv()
            total = total + self.got[i].astype(F32)
        out[...] = total
        for c in self.inner + self.outer:
            c.wait_send()


def scatter_scratch(columns):
    return [
        pltpu.VMEM((8, 64, columns), BF),
        pltpu.VMEM((7, 64, columns), BF),
        pltpu.VMEM((7, 64, columns), BF),
        DMA((15,)),
        DMA((15,)),
    ]


def small_sums_kernel(every_ref, along_ref, every_out, along_out, first, mine, got, last, ss, rs):
    dp, t = lax.axis_index("dp"), lax.axis_index("tensor")
    group = [(dp, (t + d) % 8) for d in range(1, 8)]
    line = [((dp + d) % 16, t) for d in range(1, 16)]
    greet(group + line)
    depth = every_ref.shape[1]
    copies = []
    for i, (_, to) in enumerate(group):
        c = remote(every_ref.at[to], first.at[i], ss.at[i], rs.at[i], dp, to)
        c.start()
        copies.append(c)
    total = every_ref[t]
    for i in range(7):
        copies[i].wait_recv()
        total = total + first[i]
    mine[0:depth] = total
    mine[depth : depth + along_ref.shape[0]] = along_ref[...]
    for i, (to, _) in enumerate(line):
        c = remote(mine, got.at[dp], ss.at[7 + i], rs.at[7 + i], to, t)
        c.start()
        copies.append(c)
    got[dp] = mine[...]
    for c in copies[7:22]:
        c.wait_recv()
    total = got[0]
    for i in range(1, 16):
        total = total + got[i]
    along_out[...] = total[depth : depth + along_ref.shape[0]]
    last[...] = total[0:depth]
    for i, (_, to) in enumerate(group):
        c = remote(last, every_out.at[t], ss.at[22 + i], rs.at[22 + i], dp, to)
        c.start()
        copies.append(c)
    every_out[t] = last[...]
    for c in copies[22:]:
        c.wait_recv()
    for c in copies:
        c.wait_send()


def small_sums(every, along, cid):
    a, b = every.shape[1], along.shape[0]
    return call(
        small_sums_kernel,
        "small_sums",
        cid,
        [sds(every.shape, F32), sds(along.shape, F32)],
        [
            pltpu.VMEM((7, a, 128), F32),
            pltpu.VMEM((a + b, 128), F32),
            pltpu.VMEM((16, a + b, 128), F32),
            pltpu.VMEM((a, 128), F32),
            DMA((29,)),
            DMA((29,)),
        ],
        every,
        along,
    )


def head_mask(h):
    lane = lax.broadcasted_iota(jnp.int32, (1, 2 * HD), 1)
    return (lane // HD) == h


def only_head(value, h):
    return jnp.where(head_mask(h), value, jnp.zeros_like(value))


def transposed(value):
    return value.astype(F32).T.astype(value.dtype)


def causal_block():
    key = lax.broadcasted_iota(jnp.int32, (QB, QB), 0)
    query = lax.broadcasted_iota(jnp.int32, (QB, QB), 1)
    return query >= key


def rotary_tables(positions):
    frequency = 10000.0 ** (-(jnp.arange(ROT // 2, dtype=F32) * 2.0) / ROT)
    angles = positions.astype(F32)[:, None] * frequency[None, :]
    cosine, sine = jnp.cos(angles), jnp.sin(angles)
    none = jnp.zeros_like(sine)
    rest = jnp.zeros((positions.shape[0], HD - ROT), F32)
    keep = jnp.concatenate([cosine, cosine, rest + 1.0] * 2, axis=1)
    upper = jnp.concatenate([-sine, none, rest] * 2, axis=1)
    lower = jnp.concatenate([none, sine, rest] * 2, axis=1)
    return keep, upper, lower


def turn(value, keep, upper, lower):
    return value * keep + pltpu.roll(value, 120, 1) * upper + pltpu.roll(value, 8, 1) * lower


def normalize(residual):
    mean = jnp.mean(residual, axis=1, keepdims=True)
    centered = residual - mean
    variance = jnp.mean(centered * centered, axis=1, keepdims=True)
    rstd = lax.rsqrt(variance + EPS)
    return centered * rstd, rstd


def chunk(slot):
    return pl.ds(pl.multiple_of(slot * 128, 128), 128)


def attend(core, q_ref, k_ref, v_ref, kp_ref, vp_ref, o_ref, lse_ref, o_t, v_t, vp_t):
    v_t[...] = transposed(v_ref[...])

    def block(j, earlier):
        cols = pl.ds(j * QB, QB)
        q_rows = q_ref[cols, :]
        for h in range(2):
            q_head = only_head(q_rows, h)
            heads = pl.ds(h * HD, HD)
            parts = []
            if earlier:
                parts += [
                    (dot(kp_ref[pl.ds(i * 512, 512), :], q_head, NT), vp_t[heads, pl.ds(i * 512, 512)])
                    for i in range(2)
                ]
            if j:
                parts.append((dot(k_ref[0 : j * QB, :], q_head, NT), v_t[heads, 0 : j * QB]))
            diagonal = jnp.where(causal_block(), dot(k_ref[cols, :], q_head, NT), MASKED)
            parts.append((diagonal, v_t[heads, cols]))
            top = functools.reduce(jnp.maximum, [jnp.max(s, axis=0, keepdims=True) for s, _ in parts])
            total, out = 0.0, 0.0
            for s, values in parts:
                weight = jnp.exp(s - top)
                total = total + jnp.sum(weight, axis=0, keepdims=True)
                out = out + dot(values, weight.astype(BF))
            o_t[heads, cols] = out / total
            lse_ref[h : h + 1, cols] = top + jnp.log(total)

    @pl.when(core == 1)
    def _():
        vp_t[...] = transposed(vp_ref[...])
        for j in range(ROWS // QB):
            block(j, True)

    @pl.when(core == 0)
    def _():
        for j in range(ROWS // QB):
            block(j, False)

    o_ref[...] = o_t[...].T.astype(BF)


def forward_kernel(first, *refs):
    refs = list(refs)

    def take(n):
        out = refs[:n]
        del refs[:n]
        return out

    res, gains, shifts, qkv_b, up_b, out_b, keep, upper, lower = take(9)
    wa, wb, wa_next, wb_next = take(4) if first else take(2) + [None, None]
    nrows, q, k, v, kp, vp, lse, att, act, slope, res_out = take(11)
    if first:
        shards = [wa, wb, wa_next, wb_next]
        wa, wb, wa_next, wb_next = wholes = take(4)
    o_t, v_t, vp_t, out_s, got_s, ag_s, ag_r, rs_s, rs_r, kv_s, kv_r = take(11)
    dp, t = place()
    core = dp % 2
    peers = group_peers(dp, t) + [(sibling_of(dp), t)]
    if first:
        peers += weight_peers(dp, t)
        sems = [take(2) for _ in range(4)]
        gathers = [WeightsGather(s, w, *m) for s, w, m in zip(shards, wholes, sems)]
    greet(peers)
    if first:
        gathers[0].start()
    normed, _ = normalize(res[...])
    nrows[t] = normed.astype(BF)
    rows = RowsGather(nrows, ag_s, ag_r)
    slots = rows.start()
    kv_copies = []

    def project(slot):
        where = chunk(slot)
        wide = nrows[slot].astype(F32)
        attn_in = (wide * gains[0:1] + shifts[0:1]).astype(BF)
        mlp_in = (wide * gains[1:2] + shifts[1:2]).astype(BF)
        projected = dot(attn_in, wa[:, 0:384]) + qkv_b[...]
        tables = keep[where, :], upper[where, :], lower[where, :]
        q[where, :] = (turn(projected[:, 0:128], *tables) * SCALE).astype(BF)
        k[where, :] = turn(projected[:, 128:256], *tables).astype(BF)
        v[where, :] = projected[:, 256:384].astype(BF)
        i = len(kv_copies)
        pair = [
            remote(a.at[where, :], b.at[where, :], kv_s.at[i + n], kv_r.at[i + n], sibling_of(dp), t)
            for n, (a, b) in enumerate(((k, kp), (v, vp)))
        ]
        kv_copies.extend(pair)

        @pl.when(core == 0)
        def _():
            for c in pair:
                c.start()

        hidden = dot(mlp_in, wa[:, 384:896]) + up_b[...]
        cdf = 0.5 * (1.0 + lax.erf(hidden * (0.5**0.5)))
        act[where, :] = (hidden * cdf).astype(BF)
        slope[where, :] = (cdf + hidden * (jnp.exp(-0.5 * hidden * hidden) * 0.3989422804014327)).astype(BF)

    if first:
        gathers[0].second()
        slots += rows.second()
        gathers[1].start()
        slots += rows.third()
        gathers[0].third()
        slots += rows.fourth()
        gathers[0].fourth()
        gathers[1].second()
        slots += rows.fifth()
        slots += rows.sixth()
        gathers[0].finish()
        for n, slot in enumerate(slots):
            project(slot)
            if n == 3:
                gathers[1].third()
        gathers[1].fourth()
        gathers[2].start()
        gathers[3].start()
    else:
        stages = [rows.second, rows.third, rows.fourth, rows.fifth, rows.sixth]
        for stage in stages:
            arrived = stage()
            for slot in slots:
                project(slot)
            slots = arrived
        for slot in slots:
            project(slot)

    @pl.when(core == 1)
    def _():
        for c in kv_copies:
            c.wait_recv()

    attend(core, q, k, v, kp, vp, att, lse, o_t, v_t, vp_t)
    if first:
        gathers[1].finish()
        gathers[2].second()
        gathers[3].second()

    def branch(slot):
        where = chunk(slot)
        return dot(att[where, :], wb[:, 0:128], NT) + dot(act[where, :], wb[:, 128:640], NT)

    scatter = RowsScatter(out_s, got_s, rs_s, rs_r)
    for i, (_, to) in enumerate(scatter.peers):
        scatter.send(i, branch(to))
    own = branch(t) + res[...] + out_b[...]
    if first:
        gathers[2].third()
        gathers[2].fourth()
        gathers[3].third()
        gathers[3].fourth()
    res_out[...] = scatter.finish(own)
    rows.finish()

    @pl.when(core == 0)
    def _():
        for c in kv_copies:
            c.wait_send()

    if first:
        gathers[2].finish()
        gathers[3].finish()
        for g in gathers:
            g.drain()


def forward(first, cid, *args):
    low, wide = sds((ROWS, 128), BF), sds((ROWS, 512), BF)
    out = [sds((8, 128, D), BF), low, low, low, low, low, sds((2, ROWS), F32), low, wide, wide, sds((128, D), F32)]
    scratch = [
        pltpu.VMEM((128, ROWS), F32),
        pltpu.VMEM((128, ROWS), BF),
        pltpu.VMEM((128, ROWS), BF),
        pltpu.VMEM((7, 128, D), BF),
        pltpu.VMEM((7, 128, D), BF),
        DMA((9,)),
        DMA((9,)),
        DMA((7,)),
        DMA((7,)),
        DMA((16,)),
        DMA((16,)),
    ]
    if first:
        out += [sds((D, 896), BF), sds((D, 640), BF)] * 2
        scratch += [DMA((15,))] * 8
    return call(functools.partial(forward_kernel, first), "forward", cid, out, scratch, *args)


def backward_kernel(*refs):
    refs = list(refs)

    def take(n):
        out = refs[:n]
        del refs[:n]
        return out

    grad, res, gains, affine, keep, upper, lower, wa, wb = take(9)
    nrows, q, k, v, kp, vp, lse, att, act, slope = take(10)
    grad_out, grad_a, grad_b, columns, out_b_part, along = take(6)
    grows, g_t, n_t, do, hg, pg, part_a, part_b = take(8)
    dq_t, k_t, kp_t, delta, dk, dv, dkp, dvp, dkv_out, dkv_in = take(10)
    out_s, got_s, ag_s, ag_r, rs_s, rs_r, kv_s, kv_r = take(8)
    scatter_a = WeightsScatter(part_a, *take(5))
    scatter_b = WeightsScatter(part_b, *take(5))
    dp, t = place()
    core = dp % 2
    greet(group_peers(dp, t) + [(sibling_of(dp), t)] + chip_peers(dp, t))
    grows[t] = grad[...].astype(BF)
    rows = RowsGather(grows, ag_s, ag_r)
    slots = rows.start()
    out_b_part[...] = jnp.sum(grad[...], axis=0, keepdims=True)
    k_t[...] = transposed(k[...])

    def enter(slot):
        where = chunk(slot)
        g = grows[slot]
        both = dot(g, wb[...])
        do[where, :] = both[:, 0:128].astype(BF)
        hg[where, :] = (both[:, 128:640].astype(BF).astype(F32) * slope[where, :].astype(F32)).astype(BF)
        g_t[:, where] = transposed(g)
        n_t[:, where] = transposed(nrows[slot])

    for stage in [rows.second, rows.third, rows.fourth, rows.fifth, rows.sixth]:
        arrived = stage()
        for slot in slots:
            enter(slot)
        slots = arrived
    for slot in slots:
        enter(slot)

    hg_sum = jnp.sum(hg[...].astype(F32), axis=0, keepdims=True)
    along[:, 384:896] = hg_sum

    def norm_terms(rows_of, which, weights, product, total):
        weights = weights.astype(F32)
        columns[rows_of, which : which + 1] = jnp.sum(weights * product, axis=1, keepdims=True)
        columns[rows_of, which + 2 : which + 3] = jnp.sum(weights * total, axis=1, keepdims=True)
        scale, offset = affine[rows_of, which : which + 1], affine[rows_of, which + 2 : which + 3]
        return (product * scale + total * offset).astype(BF)

    @pl.loop(0, 4)
    def _(i):
        at = pl.ds(pl.multiple_of(i * 256, 256), 256)
        product = dot(n_t[at, :], hg[...])
        part_b[at, 0:512] = norm_terms(at, 1, wa[at, 384:896], product, hg_sum)
        part_b[at, 512:640] = dot(g_t[at, :], att[...]).astype(BF)
        part_b[at, 640:1152] = dot(g_t[at, :], act[...]).astype(BF)

    scatter_b.start()

    product = (do[...].astype(F32) * att[...].astype(F32)).T
    for h in range(2):
        delta[h : h + 1, :] = jnp.sum(product[h * HD : (h + 1) * HD], axis=0, keepdims=True)
    dq_t[...] = jnp.zeros_like(dq_t)
    dk[...] = jnp.zeros_like(dk)
    dv[...] = jnp.zeros_like(dv)

    def block(j, earlier):
        cols = pl.ds(j * QB, QB)
        q_rows, do_rows = q[cols, :], do[cols, :]
        q_heads = [only_head(q_rows, h) for h in range(2)]
        do_heads = [only_head(do_rows, h) for h in range(2)]
        q_both = jnp.concatenate(q_heads, axis=0)
        do_both = jnp.concatenate(do_heads, axis=0)

        def part(keys, values, turned, dk_acc, dv_acc, at, masked):
            key_rows, value_rows = keys[at, :], values[at, :]
            probs, slopes = [], []
            for h in range(2):
                s = dot(key_rows, q_heads[h], NT)
                p = jnp.exp(s - lse[h : h + 1, cols])
                if masked:
                    p = jnp.where(causal_block(), p, 0.0)
                dprob = dot(value_rows, do_heads[h], NT)
                ds = (p * (dprob - delta[h : h + 1, cols])).astype(BF)
                heads = pl.ds(h * HD, HD)
                dq_t[heads, cols] += dot(turned[heads, at], ds)
                probs.append(p.astype(BF))
                slopes.append(ds)
            dv_acc[at, :] += dot(jnp.concatenate(probs, axis=1), do_both)
            dk_acc[at, :] += dot(jnp.concatenate(slopes, axis=1), q_both)

        if earlier:
            for i in range(ROWS // 512):
                part(kp, vp, kp_t, dkp, dvp, pl.ds(i * 512, 512), False)
        else:
            for i in range(j):
                part(k, v, k_t, dk, dv, pl.ds(i * QB, QB), False)
            part(k, v, k_t, dk, dv, cols, True)

    block(0, False)
    scatter_b.second()
    back = [
        remote(dkv_out.at[n], dkv_in.at[n], kv_s.at[n], kv_r.at[n], sibling_of(dp), t) for n in range(2)
    ]

    @pl.when(core == 1)
    def _():
        kp_t[...] = transposed(kp[...])
        dkp[...] = jnp.zeros_like(dkp)
        dvp[...] = jnp.zeros_like(dvp)
        for j in range(ROWS // QB):
            block(j, True)
        dkv_out[0] = dkp[...].astype(BF)
        dkv_out[1] = dvp[...].astype(BF)
        for c in back:
            c.start()

    for j in range(1, ROWS // QB):
        block(j, False)

    @pl.when(core == 0)
    def _():
        for n, (c, acc) in enumerate(zip(back, (dk, dv))):
            c.wait_recv()
            acc[...] += dkv_in[n].astype(F32)

    tables = keep[...], -upper[...], -lower[...]
    pg[:, 0:128] = turn(dq_t[...].T * SCALE, *tables).astype(BF)
    pg[:, 128:256] = turn(dk[...], *tables).astype(BF)
    pg[:, 256:384] = dv[...].astype(BF)

    def inward(slot):
        where = chunk(slot)
        attn_back = dot(pg[where, :], wa[:, 0:384], NT)
        mlp_back = dot(hg[where, :], wa[:, 384:896], NT)
        return attn_back * gains[0:1] + mlp_back * gains[1:2]

    scatter = RowsScatter(out_s, got_s, rs_s, rs_r)
    for i, (_, to) in enumerate(scatter.peers):
        scatter.send(i, inward(to))
    own = inward(t)

    pg_sum = jnp.sum(pg[...].astype(F32), axis=0, keepdims=True)
    along[:, 0:384] = pg_sum

    @pl.loop(0, 4)
    def _(i):
        at = pl.ds(pl.multiple_of(i * 256, 256), 256)
        product = dot(n_t[at, :], pg[...])
        part_a[at, :] = norm_terms(at, 0, wa[at, 0:384], product, pg_sum)

    scatter_a.start()
    scatter_a.second()
    normed, rstd = normalize(res[...])
    normed_grad = scatter.finish(own)
    grad_out[...] = grad[...] + rstd * (
        normed_grad
        - jnp.mean(normed_grad, axis=1, keepdims=True)
        - normed * jnp.mean(normed_grad * normed, axis=1, keepdims=True)
    )
    scatter_b.finish(grad_b)
    scatter_a.finish(grad_a)
    rows.finish()

    @pl.when(core == 1)
    def _():
        for c in back:
            c.wait_send()


def backward(cid, *args):
    vm = pltpu.VMEM
    out = [
        sds((128, D), F32), sds((64, 384), F32), sds((64, 1152), F32), sds((D, 4), F32), sds((1, D), F32), sds((1, 896), F32)
    ]
    scratch = [
        vm((8, 128, D), BF), vm((D, ROWS), BF), vm((D, ROWS), BF), vm((ROWS, 128), BF), vm((ROWS, 512), BF),
        vm((ROWS, 384), BF), vm((D, 384), BF), vm((D, 1152), BF),
        vm((128, ROWS), F32), vm((128, ROWS), BF), vm((128, ROWS), BF), vm((2, ROWS), F32),
        vm((ROWS, 128), F32), vm((ROWS, 128), F32), vm((ROWS, 128), F32), vm((ROWS, 128), F32),
        vm((2, ROWS, 128), BF), vm((2, ROWS, 128), BF),
        vm((7, 128, D), BF), vm((7, 128, D), BF),
        DMA((9,)), DMA((9,)), DMA((7,)), DMA((7,)), DMA((2,)), DMA((2,)),
    ] + scatter_scratch(384) + scatter_scratch(1152)
    return call(backward_kernel, "backward", cid, out, scratch, *args)


def local(
    tokens, qkv_weight, qkv_bias, out_weight, up_weight, up_bias, down_weight,
    norm_gain, norm_shift, out_bias, cotangent,
):
    core = lax.axis_index("dp") % 2
    tables = rotary_tables(core * ROWS + jnp.arange(ROWS, dtype=jnp.int32))
    gains, shifts = norm_gain.astype(F32), norm_shift.astype(F32)
    affine = jnp.concatenate([gains, shifts], axis=1).transpose(0, 2, 1)
    shards = []
    for l in range(LAYERS):
        shards.append(jnp.concatenate([qkv_weight[l].reshape(64, 384), up_weight[l]], axis=1))
        shards.append(jnp.concatenate([out_weight[l], down_weight[l]], axis=1))
    residual = tokens.astype(F32)
    weights = shards
    saved = []
    for l in range(LAYERS):
        out = forward(
            l == 0, l, residual, gains[l], shifts[l],
            qkv_bias[l].astype(F32).reshape(1, 384), up_bias[l].astype(F32).reshape(1, 512),
            out_bias[l].astype(F32).reshape(1, D), *tables,
            *(weights if l == 0 else weights[2:]),
        )
        if l == 0:
            weights = out[11:]
        saved.append((residual, out[:10]))
        residual = out[10]
    output = residual.astype(BF)
    grad = cotangent.astype(F32)
    grads = [None] * LAYERS
    along = [None] * LAYERS
    every = [None] * LAYERS
    for l in reversed(range(LAYERS)):
        layer_in, kept = saved[l]
        grad, grad_a, grad_b, columns, out_b_part, along[l] = backward(
            2 + l, grad, layer_in, gains[l], affine[l], *tables, weights[2 * l], weights[2 * l + 1], *kept
        )
        grads[l] = (grad_a, grad_b)
        every[l] = jnp.concatenate([columns.T, out_b_part], axis=0)
    every_sum, along_sum = small_sums(
        jnp.stack(every).reshape(8, 10, 128), jnp.stack(along).reshape(14, 128), 4
    )
    every_sum = every_sum.reshape(LAYERS, 5, D)
    along_sum = along_sum.reshape(LAYERS, 896)
    grad_a = jnp.stack([g[0] for g in grads])
    grad_b = jnp.stack([g[1] for g in grads])
    return (
        output,
        grad,
        grad_a.reshape(LAYERS, 64, 3, 128),
        along_sum[:, 0:384].reshape(LAYERS, 3, 128),
        grad_b[:, :, 512:640],
        grad_b[:, :, 0:512],
        along_sum[:, 384:896],
        grad_b[:, :, 640:1152],
        every_sum[:, 0:2],
        every_sum[:, 2:4],
        every_sum[:, 4],
    )


def solution(mesh):
    in_specs = (
        P(("dp", "tensor"), None),
        P(None, "dp", None, "tensor"),
        P(None, None, "tensor"),
        P(None, "dp", "tensor"),
        P(None, "dp", "tensor"),
        P(None, "tensor"),
        P(None, "dp", "tensor"),
        P(),
        P(),
        P(),
        P(("dp", "tensor"), None),
    )
    out_specs = (
        P(("dp", "tensor"), None),
        P(("dp", "tensor"), None),
        P(None, "dp", None, "tensor"),
        P(None, None, "tensor"),
        P(None, "dp", "tensor"),
        P(None, "dp", "tensor"),
        P(None, "tensor"),
        P(None, "dp", "tensor"),
        P(),
        P(),
        P(),
    )
    return jax.shard_map(local, mesh=mesh, in_specs=in_specs, out_specs=out_specs, check_vma=False)
```

time: 596 us -> 366 us (0.61)
  Pallas kernels: 416 us -> 328 us
  matrix products: 70.2 us -> 0 us
  other arithmetic: 44.7 us -> 14.8 us
  local copies, waits for them, and re-layouts: 40.1 us -> 15 us
  starting transfers between devices: 13.4 us -> 0 us
    pallas_call x17 -> x5, Pallas kernels: 416 us -> 328 us  [call(): pl.pallas_call(kernel, name=name, out_shape=out, in_specs=[VM] * len(args...]
    dot_general x24 -> x0, matrix products: 70.2 us -> none  [dot(): return lax.dot_general(a, b, dims, preferred_element_type=F32)]
    ppermute x4 -> x0, starting transfers between devices: 13.4 us -> none  [the longest x2 10.9 us: local(): back_k, back_v = lax.ppermute(jnp.stack([dkp, dvp]), 'dp', PAIR_DOWN)]
    slice x16 -> x0, local copies, waits for them, and re-layouts: 10.2 us -> none  [the longest x8 4.76 us: turn_back(): jnp.roll(value, 8, axis=1) * lower]
    concatenate x2 -> x1, local copies, waits for them, and re-layouts: 9.28 us -> 0.36 us  [local(): affine = jnp.concatenate([gains, shifts], axis=1).transpose(0, 2, 1)]
    reduce_sum x9 -> x0, other arithmetic: 8.65 us -> none  [the longest x2 2.53 us: local(): jnp.mean(normed_grad, axis=1, keepdims=True)]
    another operation x8 -> x2, other arithmetic: 8.4 us -> 0.91 us  [the longest x1 0.85 us: local(): grad_b = jnp.stack([g[1] for g in grads])]
  transfers between devices with their start and end apart: 4 -> 0, of which waited for: 0 -> 0; matrix products, arithmetic and copies ran while one was open for 7% -> 0% of each run, Pallas kernels for 14% -> 0%
where the time goes in v2:
time: 366 us; the launch traced here: 359 us
  Pallas kernels  328 us (90%)
  local copies, waits for them, and re-layouts  15 us (4%)
  other arithmetic  14.8 us (4%)
    pallas_call x5, Pallas kernels, call(): pl.pallas_call(kernel, name=name, out_shape=out, in_specs=[VM] * len(args...  328 us

profile of v2, /device:TPU:1, one launch (start us, length us, event | category | flops | bytes accessed | tf_op | source)
XLA Modules:
  0.0 358.8 jit_solution(12397699016920198751)
XLA Ops:
  0.6 1.8 convert_element_type.64.refs_0_.refs_1_
  2.4 0.7 convert_element_type.66
  3.1 0.7 convert_element_type.65
  3.8 0.6 slice_bitcast_fusion.8
  4.5 1.3 bitcast_convert_fusion
  5.8 1.3 slice_convert_fusion.2
  7.1 1.4 slice_convert_fusion
  8.5 1.9 multiply_sine_fusion
  10.5 1.8 concatenate.31.refs_6_.refs_4_
  12.3 1.7 concatenate.32.refs_7_.refs_5_
  14.1 1.8 concatenate.33.refs_8_.refs_6_
  15.9 0.0 copy-done.6
  15.9 0.0 copy-done.9
  16.0 0.7 pad_maximum_fusion.3
  16.8 0.0 copy-done.7
  16.8 0.0 copy-done.11
  16.8 0.7 pad_maximum_fusion.5
  17.5 82.3 %forward.2 = (bf16[8,128,1024]{2,1,0:T(8,128)(2,1)}, bf16[1024,128]{1,0:T(8,128)(2,1)}, bf16[1024,128]{1,0:T(8,128)(2,1)}, bf16[1024,128]{1,0:T(8,128)(2,1)}, bf...) custom-call(f32[128,1024]{1,0:T(8,128)} %convert_element_type.64.ref, ...), custom_call_target="tpu_custom_call" | custom-call | tf_op jit(solution)/shard_map/forward/pallas_call | solution.py:52
  99.8 0.0 copy-start.5
  99.8 68.5 %forward.3 = (bf16[8,128,1024]{2,1,0:T(8,128)(2,1)}, bf16[1024,128]{1,0:T(8,128)(2,1)}, bf16[1024,128]{1,0:T(8,128)(2,1)}, bf16[1024,128]{1,0:T(8,128)(2,1)}, bf...) custom-call(f32[128,1024]{1,0:T(8,128)} %get-tuple-element.51.refs_0, ...), custom_call_target="tpu_custom_call" | custom-call | tf_op jit(solution)/shard_map/forward/pallas_call | solution.py:52
  168.3 1.8 convert_element_type.76
  170.0 0.0 copy-done.5
  170.0 0.8 convert_element_type.77.refs_0_
  170.9 0.4 copy.70
  171.3 1.1 slice_bitcast_fusion
  172.3 80.8 %backward.2 = (f32[128,1024]{1,0:T(8,128)}, f32[64,384]{1,0:T(8,128)}, f32[64,1152]{1,0:T(8,128)}, f32[1024,4]{1,0:T(8,128)}, f32[1,1024]{1,0:T(1,128)}, /*index=5*/f32[1,896]{1,0:T(1,128)}) custom-call(f32[128,1024]{1,0:T(8,128)} %convert_element_type.77.refs_0_, f32[128,1024]{1,0:T(8,128)} %get-tuple-element.51.refs_0_.refs_1_, ...), custom_call_target="tpu_custom_call" | custom-call | tf_op jit(solution)/shard_map/backward/pallas_call | solution.py:52
  253.2 0.0 copy-start.8
  253.2 0.0 copy-start.3
  253.2 78.4 %backward.3 = (f32[128,1024]{1,0:T(8,128)}, f32[64,384]{1,0:T(8,128)}, f32[64,1152]{1,0:T(8,128)}, f32[1024,4]{1,0:T(8,128)}, f32[1,1024]{1,0:T(1,128)}, /*index=5*/f32[1,896]{1,0:T(1,128)}) custom-call(f32[128,1024]{1,0:T(8,128)} %get-tuple-element.65.refs_0_, f32[128,1024]{1,0:T(8,128)} %convert_element_type.64.refs_0_.refs_1_, ...), custom_call_target="tpu_custom_call" | custom-call | tf_op jit(solution)/shard_map/backward/pallas_call | solution.py:52
  331.7 1.0 stack.36
  332.7 0.1 pad_maximum_fusion.2
  332.8 0.7 copy.73
  333.5 0.2 copy.72
  333.7 0.2 copy.71
  333.9 0.6 reshape.84.every_ref
  334.6 0.6 reshape.85.along_ref
  335.2 17.7 %small_sums.1 = (f32[8,10,128]{2,1,0:T(8,128)}, f32[14,128]{1,0:T(8,128)}) custom-call(f32[8,10,128]{2,1,0:T(8,128)} %reshape.84.every_ref, f32[14,128]{1,0:T(8,128)} %reshape.85.along_ref), custom_call_target="tpu_custom_call" | custom-call | tf_op jit(solution)/shard_map/small_sums/pallas_call | solution.py:52
  352.9 0.7 reshape.86
  353.7 0.6 slice_bitcast_fusion.12
  354.3 0.0 copy-done
  354.3 0.6 pad_maximum_fusion.7
  354.9 0.8 pad_maximum_fusion
  355.8 0.6 slice.121
  356.3 0.0 copy-done.10
  356.4 0.6 fusion.2
  357.0 0.6 copy.82
  357.6 0.0 copy-done.2
  357.6 0.8 copy.84
  (42 shorter events, 0.4 us)
Async XLA Ops:
  14.1 1.8 copy-start.6
  14.1 1.8 copy-start.9
  14.1 2.7 copy-start.7
  14.1 2.7 copy-start.11
  99.8 70.3 %copy-start.5 = (bf16[128,1024]{1,0:T(8,128)(2,1)S(1)}, bf16[128,1024]{1,0:T(8,128)(2,1)}, u32[]{:S(2)}) copy-start(bf16[128,1024]{1,0:T(8,128)(2,1)} %param.21) | copy-start | bytes 786436
  253.2 78.5 %copy-start.8 = (f32[64,384]{1,0:T(8,128)S(1)}, f32[64,384]{1,0:T(8,128)}, u32[]{:S(2)}) copy-start(f32[64,384]{1,0:T(8,128)} %get-tuple-element.80) | copy-start | bytes 294916
  253.2 80.3 %copy-start.3 = (f32[1024,4]{1,0:T(8,128)S(1)}, f32[1024,4]{1,0:T(8,128)}, u32[]{:S(2)}) copy-start(f32[1024,4]{1,0:T(8,128)} %get-tuple-element.83) | copy-start | bytes 49156
  331.6 2.1 copy-start.12
  331.6 2.1 copy-start.4
  331.6 2.3 copy-start.13
  331.6 3.0 copy-start.14
  331.6 3.0 copy-start.15
  331.6 22.6 %copy-start = (f32[64,1152]{1,0:T(8,128)S(1)}, f32[64,1152]{1,0:T(8,128)}, u32[]{:S(2)}) copy-start(f32[64,1152]{1,0:T(8,128)} %get-tuple-element.89) | copy-start | bytes 884740
  331.6 22.6 %copy-start.1 = (f32[64,1152]{1,0:T(8,128)S(1)}, f32[64,1152]{1,0:T(8,128)}, u32[]{:S(2)}) copy-start(f32[64,1152]{1,0:T(8,128)} %get-tuple-element.88) | copy-start | bytes 884740
  333.5 24.1 %copy-start.2 = (f32[128,1024]{1,0:T(8,128)S(1)}, f32[128,1024]{1,0:T(8,128)}, u32[]{:S(2)}) copy-start(f32[128,1024]{1,0:T(8,128)} %get-tuple-element.180) | copy-start | bytes 1572868
  352.9 3.4 copy-start.10
